TPU v7x, 256 devices: a whole 4x4x8 slice. The times are simulated.
256 devices in a mesh: depth: 32 (over y, z), col: 8 (over x, core).
Axes of the slice: x: 4, y: 4, z: 8, core: 2. Of those that a mesh axis runs over, the one named last changes fastest.
Arguments:
- volume: float32 [512, 256, 2048], P('depth', None, 'col'), may hold values from -6 to 6
- tf_center: float32 [8], replicated, may hold values from -2.5 to 2.5
- tf_width: float32 [8], replicated, may hold values from 0.3 to 1.5
- tf_density: float32 [8], replicated, may hold values from 0.1 to 2
- tf_color: float32 [3, 8], replicated, may hold values from 0.05 to 1
- light: float32 [3], replicated, may hold values from 0.3 to 1
Outputs:
- image: float32 [4, 256, 2048], P(None, 'depth', 'col')
All inputs are finite; a program needn't handle non-finite values.
Results may differ from a plain program's by a relative error of at most 0.00028.
Values sent between devices are 32-bit elements; how exact they have to be, the bound alone decides.
No kernel may reach another device: no remote copies, remote signals or barrier semaphores. Data moves between devices by JAX's collectives and lax.ppermute only.
A program may use at most 64 MiB of HBM per device.

v0:
```python
import jax
import jax.numpy as jnp
from jax import lax
from jax.sharding import PartitionSpec as P


def with_halo(array, sides, width):
    for axis, dim in sides:
        size, length = (lax.axis_size(axis), array.shape[dim])
        up = [(i, (i + 1) % size) for i in range(size - 1)]
        down = [(j, i) for i, j in up]
        last = lax.slice_in_dim(array, length - width, length, axis=dim)
        leading = lax.slice_in_dim(array, 0, width, axis=dim)
        before = lax.ppermute(last, axis, up)
        after = lax.ppermute(leading, axis, down)
        array = jnp.concatenate([before, array, after], axis=dim)
    return array


def prefix(array, axis, combine, identity):
    length, place = (lax.axis_size(axis), lax.axis_index(axis))
    everything = lax.all_gather(array, axis)
    start = jnp.broadcast_to(jnp.asarray(identity, array.dtype), array.shape)

    def step(k, before):
        reached = k < place
        new = combine(before, everything[k])
        return jnp.where(reached, new, before)

    return lax.fori_loop(0, length, step, start)


def classify(cell, tf_center, tf_width, tf_density, tf_color, depth_all):
    bumps = jnp.exp(-jnp.square((cell[None] - tf_center[:, None, None]) / tf_width[:, None, None]))
    ext = jnp.sum(tf_density[:, None, None] * bumps, axis=0) / depth_all
    emit = jnp.einsum("ck,kyx->cyx", tf_color, bumps, precision=lax.Precision.HIGHEST)
    return (ext, emit)


def on_device(volume, tf_center, tf_width, tf_density, tf_color, light):
    depth_local = volume.shape[0]
    depth_all = depth_local * lax.axis_size("depth")
    padded = with_halo(volume, (("depth", 0), ("col", 2)), 1)

    def march(carry, index):
        color, optical = carry
        slabs = lax.dynamic_slice_in_dim(padded, index, 3, 0)
        middle = jnp.pad(slabs[1], ((1, 1), (0, 0)))
        cell = middle[1:-1, 1:-1]
        grad_x = (middle[1:-1, 2:] - middle[1:-1, :-2]) * 0.5
        grad_y = (middle[2:, 1:-1] - middle[:-2, 1:-1]) * 0.5
        grad_z = (slabs[2, :, 1:-1] - slabs[0, :, 1:-1]) * 0.5
        lit = jnp.abs(light[0] * grad_x + light[1] * grad_y + light[2] * grad_z)
        shade = 0.3 + 0.7 * lit / jnp.sqrt(
            grad_x * grad_x + grad_y * grad_y + grad_z * grad_z + 1.0
        )
        ext, emit = classify(cell, tf_center, tf_width, tf_density, tf_color, depth_all)
        weight = jnp.exp(-optical) * (1.0 - jnp.exp(-ext)) * shade
        return ((color + weight[None] * emit, optical + ext), None)

    rows_all = volume.shape[1]
    cols = volume.shape[2]
    start = (jnp.zeros((3, rows_all, cols), jnp.float32), jnp.zeros((rows_all, cols), jnp.float32))
    (color, optical), unused = lax.scan(march, start, jnp.arange(depth_local, dtype=jnp.int32))
    before = prefix(
        optical, "depth", lambda earlier, later: earlier + later, jnp.zeros_like(optical)
    )
    terms = jnp.concatenate([jnp.exp(-before)[None] * color, optical[None]], axis=0)
    owned = lax.psum_scatter(terms, "depth", scatter_dimension=1, tiled=True)
    total_color = owned[:3]
    total_optical = owned[3]
    return jnp.concatenate([total_color, (1.0 - jnp.exp(-total_optical))[None]], axis=0)


def solution(mesh):
    return jax.shard_map(
        on_device,
        mesh=mesh,
        in_specs=(P("depth", None, "col"), P(), P(), P(), P(), P()),
        out_specs=P(None, "depth", "col"),
        check_vma=False,
    )
```

profile of v0, /device:TPU:4, one launch (start us, length us, event | category | flops | bytes accessed | tf_op | source)
XLA Modules:
  0.0 551.6 jit_solution(12297545123826803341)
XLA Ops:
  6.5 5.4 copy.8
  13.0 3.8 collective-permute-start
  16.9 1.3 collective-permute-start.1
  18.2 4.2 collective-permute-done
  22.4 4.3 collective-permute-done.1
  27.7 1.9 collective-permute-start.2
  29.6 3.6 collective-permute-start.3
  36.1 4.2 pad_maximum_fusion
  40.3 153.5 %while.29 = (s32[]{:T(128)}, f32[3,256,256]{2,0,1:T(4,128)S(1)}, f32[256,256]{1,0:T(8,128)S(1)}, f32[8]{0:T(128)S(1)}, s32[16]{0:T(128)S(1)}, /*index=5*/f32[18,...) while((s32[]{:T(128)}, f32[3,256,256]{2,0,1:T(4,128)S(1)}, ...), condition=%wide.region_2.3_spmd.clone, body=%wide.region_0.2_spmd.clone.sunk | while | flops 26542088 | bytes 8790550 | solution.py:64
  42.8 1.1 constant_dynamic-slice_fusion.6
  46.9 3.0 fusion.23
  52.4 1.1 constant_dynamic-slice_fusion.6
  56.5 3.0 fusion.23
  62.0 1.1 constant_dynamic-slice_fusion.6
  66.1 3.0 fusion.23
  71.6 1.1 constant_dynamic-slice_fusion.6
  75.7 3.0 fusion.23
  85.3 3.0 fusion.23
  94.9 3.0 fusion.23
  104.5 3.0 fusion.23
  114.0 3.0 fusion.23
  123.6 3.0 fusion.23
  133.2 3.0 fusion.23
  142.8 3.0 fusion.23
  152.4 3.0 fusion.23
  162.0 3.0 fusion.23
  171.6 3.0 fusion.23
  181.2 3.0 fusion.23
  190.8 3.0 fusion.23
  194.7 101.2 %all-gather.3.cloned.1.call-done = f32[8192,256]{1,0:T(8,128)} async-done(((f32[256,256]{1,0:T(8,128)}), f32[8192,256]{1,0:T(8,128)}) %all-gather.3.cloned.1.call-update) | async-done | bytes 8388624 | tf_op jit(solution)/shard_map/all_gather | solution.py:22
  295.8 33.8 %while.30 = (s32[]{:T(128)}, f32[256,256]{1,0:T(8,128)S(1)}, s32[]{:T(128)}, f32[32,256,256]{2,1,0:T(8,128)}, s32[]{:T(128)}, /*index=5*/s32[]{:T(128)}) while((s32[]{:T(128)}, f32[256,256]{1,0:T(8,128)S(1)}, s32[]{:T(128)}, f32[32,256,256]{2,1,0:T(8,128)}, s32[]{:T(128)}, /*index=5*/s32[]{:T(128)}) %tuple.78), condition=%wide.region_4.5_spmd.clone, body=%wide.region_3.4_spmd.clone.sunk | while | flops 196612 | bytes 786525 | solution.py:30
  331.0 211.7 %reduce-scatter.2.cloned.1.call-done = f32[4,8,256]{2,1,0:T(8,128)} async-done(((f32[4,256,256]{2,1,0:T(8,128)}), f32[4,8,256]{2,1,0:T(8,128)}) %reduce-scatter.2.cloned.1.call-update) | async-done | bytes 32784 | tf_op jit(solution)/shard_map/reduce_scatter | solution.py:69
  (205 shorter events, 109.1 us)
Async XLA Ops:
  6.5 289.3 %all-gather.3.cloned.1.call-start = ((), (), s32[]{:S(2)}) async-start(), calls=%async_computation.2 | async-start | bytes 8650752 | tf_op jit(solution)/shard_map/all_gather | solution.py:22
  12.0 21.3 %copy-start.2 = (f32[3]{0:T(128)S(1)}, f32[3]{0:T(128)}, u32[]{:S(2)}) copy-start(f32[3]{0:T(128)} %param.15) | copy-start | bytes 40
  13.0 9.4 %collective-permute-start = (f32[1,256,256]{1,2,0:T(8,128)S(1)}, f32[1,256,256]{1,2,0:T(8,128)S(1)}, u32[]{:S(2)}, u32[]{:S(2)}) collective-permute-start(f32[1,256,256]{1,2,0:T(8,128)S(1)} %get-tuple-element.329), channel_id=1, source_target_pairs={{0,8},{8,16},{16,24},{24,32},{32,40},{40,48},{48,56},{56,64},{64,7... | collective-permute-start | bytes 786440 | tf_op jit(solution)/shard_map/ppermute | solution.py:14
  16.9 9.8 %collective-permute-start.1 = (f32[1,256,256]{1,2,0:T(8,128)S(1)}, f32[1,256,256]{1,2,0:T(8,128)S(1)}, u32[]{:S(2)}, u32[]{:S(2)}) collective-permute-start(f32[1,256,256]{1,2,0:T(8,128)S(1)} %get-tuple-element.330), channel_id=1, source_target_pairs={{8,0},{16,8},{24,16},{32,24},{40,32},{48,40},{56,48},{64,56},{72,6... | collective-permute-start | bytes 786440 | tf_op jit(solution)/shard_map/ppermute | solution.py:15
  27.7 8.3 %collective-permute-start.2 = (f32[18,256,1]{1,2,0:T(1,128)S(1)}, f32[18,256,1]{1,2,0:T(1,128)S(1)}, u32[]{:S(2)}, u32[]{:S(2)}) collective-permute-start(f32[18,256,1]{1,2,0:T(1,128)S(1)} %get-tuple-element.327), channel_id=1, source_target_pairs={{0,1},{1,2},{2,3},{3,4},{4,5},{5,6},{6,7},{8,9},{9,10},{10,11},{11... | collective-permute-start | bytes 55304 | tf_op jit(solution)/shard_map/ppermute | solution.py:14
  29.6 6.4 %collective-permute-start.3 = (f32[18,256,1]{1,2,0:T(1,128)S(1)}, f32[18,256,1]{1,2,0:T(1,128)S(1)}, u32[]{:S(2)}, u32[]{:S(2)}) collective-permute-start(f32[18,256,1]{1,2,0:T(1,128)S(1)} %get-tuple-element.328), channel_id=1, source_target_pairs={{1,0},{2,1},{3,2},{4,3},{5,4},{6,5},{7,6},{9,8},{10,9},{11,10},{12... | collective-permute-start | bytes 55304 | tf_op jit(solution)/shard_map/ppermute | solution.py:15
  36.0 4.3 copy-start.3
  36.0 4.3 copy-start.4
  36.0 4.3 copy-start.5
  36.0 4.3 copy-start.6
  193.8 0.7 copy-start
  194.6 135.3 %copy-start.1 = (f32[256,256]{1,0:T(8,128)S(1)}, f32[256,256]{1,0:T(8,128)}, u32[]{:S(2)}) copy-start(f32[256,256]{1,0:T(8,128)} %copy-done) | copy-start | bytes 786436
  194.6 348.1 %reduce-scatter.2.cloned.1.call-start = ((), (), s32[]{:S(2)}) async-start(), calls=%async_computation.1 | async-start | bytes 1081344 | tf_op jit(solution)/shard_map/reduce_scatter | solution.py:69
Sparse Core Ops, SparseCore 0:
  194.7 101.0 all-gather.2
  331.1 211.4 reduce-scatter.1
where the time goes:
time: 554 us; the launch traced here: 552 us
  waiting for transfers between devices  321 us (58%)
  other arithmetic  62.8 us (11%)
  local copies, waits for them, and re-layouts  60.2 us (11%)
  matrix products  48.5 us (9%)
  loops' own time  32.4 us (6%)
  between operations  15.6 us (3%)
  starting transfers between devices  10.7 us (2%)
    reduce_scatter x1, waiting for transfers between devices, on_device(): owned = lax.psum_scatter(terms, 'depth', scatter_dimension=1, tiled=True)  212 us
    all_gather x1, waiting for transfers between devices, prefix(): everything = lax.all_gather(array, axis)  101 us
    dot_general x16, matrix products, classify(): jnp.einsum('ck,kyx->cyx', tf_color, bumps, precision=lax.Precision.HIGHEST)  48.5 us
    select_n x32, other arithmetic, step(): return jnp.where(reached, new, before)  33.1 us
    another operation x1, loops' own time, on_device(): lax.scan(march, start, jnp.arange(depth_local, dtype=jnp.int32))  31.6 us
    slice x16, local copies, waits for them, and re-layouts, march(): grad_z = (slabs[2, :, 1:-1] - slabs[0, :, 1:-1]) * 0.5  17.4 us
    slice x16, local copies, waits for them, and re-layouts, march(): middle = jnp.pad(slabs[1], ((1, 1), (0, 0)))  15.6 us
    reduce_sum x16, other arithmetic, classify(): ext = jnp.sum(tf_density[:, None, None] * bumps, axis=0) / depth_all  15.6 us
  transfers between devices with their start and end apart: 6, of which 4 were waited for; matrix products, arithmetic and copies ran while one was open for 0% of the time, Pallas kernels for 0%

commit v1 on v0

v1 whole, which is shorter than its diff:
```python
import functools
import math

import jax
import jax.numpy as jnp
from jax import lax
from jax.experimental import pallas as pl
from jax.experimental.pallas import tpu as pltpu
from jax.sharding import PartitionSpec as P

LANES = 128
SUB = 8


def march_kernel(par, vol, low, high, left, right, out, cells, sems):
    depth, rows, cols = vol.shape
    tiles = cols // LANES
    bumps = 8
    copies = []
    for t in range(tiles):
        lanes = pl.ds(t * LANES, LANES)
        for i, (src, dst) in enumerate((
            (vol.at[:, :, lanes], cells.at[t, pl.ds(1, depth), pl.ds(SUB, rows)]),
            (low.at[:, :, lanes], cells.at[t, pl.ds(0, 1), pl.ds(SUB, rows)]),
            (high.at[:, :, lanes], cells.at[t, pl.ds(depth + 1, 1), pl.ds(SUB, rows)]),
        )):
            copies.append(pltpu.make_async_copy(src, dst, sems.at[3 * t + i]))
    for copy in copies:
        copy.start()
    edge = jnp.zeros((tiles, depth + 2, SUB, LANES), jnp.float32)
    cells[:, :, pl.ds(0, SUB), :] = edge
    cells[:, :, pl.ds(SUB + rows, SUB), :] = edge
    for copy in copies:
        copy.wait()

    lane = lax.broadcasted_iota(jnp.int32, (SUB, LANES), 1)
    first = lane == 0
    last = lane == LANES - 1

    def block(rb, unused):
        base = pl.multiple_of(rb * SUB, SUB)

        def cell(t, z, shift=0):
            return cells[t, z, pl.ds(base + SUB + shift, SUB), :]

        halo_left = left[rb]
        halo_right = right[rb]
        acc = [[None] * bumps for t in range(tiles)]
        logt = [None] * tiles
        trans = [None] * tiles
        for z in range(depth):
            here = [cell(t, z + 1) for t in range(tiles)]
            fwd = [pltpu.roll(h, 1, 1) for h in here]
            bwd = [pltpu.roll(h, LANES - 1, 1) for h in here]
            lo = halo_left if z == 0 else pltpu.roll(halo_left, LANES - z, 1)
            hi = pltpu.roll(halo_right, LANES - 1 - z, 1)
            for t in range(tiles):
                v = here[t]
                from_left = jnp.where(first, lo if t == 0 else fwd[t - 1], fwd[t])
                from_right = jnp.where(last, hi if t == tiles - 1 else bwd[t + 1], bwd[t])
                dx = from_right - from_left
                dy = cell(t, z + 1, 1) - cell(t, z + 1, -1)
                dz = cell(t, z + 2) - cell(t, z)
                lit = jnp.abs(par[24] * dx + par[25] * dy + par[26] * dz)
                norm = (dx * dx + dy * dy) + (dz * dz + 4.0)
                shade = 0.3 + lit * lax.rsqrt(norm)
                b = []
                for k in range(bumps):
                    u = v - par[k]
                    b.append(jnp.exp2(u * u * par[8 + k]))
                e = [b[k] * par[16 + k] for k in range(bumps)]
                ext = ((e[0] + e[1]) + (e[2] + e[3])) + ((e[4] + e[5]) + (e[6] + e[7]))
                logt[t] = ext if z == 0 else logt[t] + ext
                after = jnp.exp2(logt[t])
                weight = ((1.0 if z == 0 else trans[t]) - after) * shade
                trans[t] = after
                for k in range(bumps):
                    term = weight * b[k]
                    acc[t][k] = term if z == 0 else acc[t][k] + term
        for t in range(tiles):
            lanes = pl.ds(t * LANES, LANES)
            for c in range(3):
                total = acc[t][0] * par[32 + c * bumps]
                for k in range(1, bumps):
                    total = total + acc[t][k] * par[32 + c * bumps + k]
                out[rb, c, :, lanes] = total
            out[rb, 3, :, lanes] = logt[t]
        return 0

    lax.fori_loop(0, rows // SUB, block, 0)


def march(par, vol, low, high, left, right):
    depth, rows, cols = vol.shape
    blocks = rows // SUB
    anywhere = pl.BlockSpec(memory_space=pl.ANY)
    return pl.pallas_call(
        march_kernel,
        out_shape=jax.ShapeDtypeStruct((blocks, 4, SUB, cols), jnp.float32),
        in_specs=[pl.BlockSpec(memory_space=pltpu.SMEM)] + [anywhere] * 3
        + [pl.BlockSpec(memory_space=pltpu.VMEM)] * 2,
        out_specs=pl.BlockSpec(memory_space=pltpu.VMEM),
        scratch_shapes=[
            pltpu.VMEM((cols // LANES, depth + 2, rows + 2 * SUB, LANES), jnp.float32),
            pltpu.SemaphoreType.DMA((3 * (cols // LANES),)),
        ],
        compiler_params=pltpu.CompilerParams(vmem_limit_bytes=32 * 1024 * 1024),
        name="march",
    )(par, vol, low, high, left, right)


def merge_kernel(parts, out):
    slabs = parts.shape[0]
    color = [parts[0, c] for c in range(3)]
    logt = parts[0, 3]
    for s in range(1, slabs):
        seen = jnp.exp2(logt)
        color = [color[c] + seen * parts[s, c] for c in range(3)]
        logt = logt + parts[s, 3]
    for c in range(3):
        out[c] = color[c]
    out[3] = 1.0 - jnp.exp2(logt)


def merge(parts):
    slabs, channels, rows, cols = parts.shape
    return pl.pallas_call(
        merge_kernel,
        out_shape=jax.ShapeDtypeStruct((channels, rows, cols), jnp.float32),
        in_specs=[pl.BlockSpec(memory_space=pltpu.VMEM)],
        out_specs=pl.BlockSpec(memory_space=pltpu.VMEM),
        name="merge",
    )(parts)


def edge_lanes(column):
    depth, rows = column.shape
    spread = column.reshape(depth, rows // SUB, SUB).transpose(1, 2, 0)
    return jnp.pad(spread, ((0, 0), (0, 0), (0, LANES - depth)))


def on_device(volume, tf_center, tf_width, tf_density, tf_color, light):
    depth, rows, cols = volume.shape
    slabs = lax.axis_size("depth")
    depth_all = depth * slabs
    up = [(i, i + 1) for i in range(slabs - 1)]
    down = [(j, i) for i, j in up]
    low = lax.ppermute(volume[depth - 1:], "depth", up)
    high = lax.ppermute(volume[:1], "depth", down)
    width = lax.axis_size("col")
    east = [(i, i + 1) for i in range(width - 1)]
    west = [(j, i) for i, j in east]
    left = lax.ppermute(volume[:, :, cols - 1], "col", east)
    right = lax.ppermute(volume[:, :, 0], "col", west)

    log2e = math.log2(math.e)
    par = jnp.concatenate([
        tf_center,
        -log2e / jnp.square(tf_width),
        tf_density * (-log2e / depth_all),
        0.7 * light,
        jnp.zeros((5,), jnp.float32),
        tf_color.reshape(-1),
    ])
    parts = march(par, volume, low, high, edge_lanes(left), edge_lanes(right))
    parts = lax.all_to_all(parts, "depth", 0, 0, tiled=True)
    return merge(parts)


def solution(mesh):
    return jax.shard_map(
        on_device,
        mesh=mesh,
        in_specs=(P("depth", None, "col"), P(), P(), P(), P(), P()),
        out_specs=P(None, "depth", "col"),
        check_vma=False,
    )
```

time: 554 us -> 85.6 us (0.15)
  waiting for transfers between devices: 321 us -> 7.8 us
  other arithmetic: 62.8 us -> 0.01 us
  local copies, waits for them, and re-layouts: 60.2 us -> 10.7 us
  matrix products: 48.5 us -> 0 us
  blocking collectives: 0 us -> 38.2 us
  loops' own time: 32.4 us -> 0 us
  Pallas kernels: 0 us -> 16.8 us
  between operations: 15.6 us -> 0.14 us
    reduce_scatter x1 -> x0, waiting for transfers between devices: 212 us -> none  [on_device(): owned = lax.psum_scatter(terms, 'depth', scatter_dimension=1, tiled=True)]
    all_gather x1 -> x0, waiting for transfers between devices: 101 us -> none  [prefix(): everything = lax.all_gather(array, axis)]
    dot_general x16 -> x0, matrix products: 48.5 us -> none  [classify(): jnp.einsum('ck,kyx->cyx', tf_color, bumps, precision=lax.Precision.HIGHEST)]
    all_to_all x0 -> x1, blocking collectives: none -> 38.2 us  [on_device(): parts = lax.all_to_all(parts, 'depth', 0, 0, tiled=True)]
    select_n x32 -> x0, other arithmetic: 33.1 us -> none  [step(): return jnp.where(reached, new, before)]
    another operation x2 -> x0, loops' own time: 32.4 us -> none  [the longest x1 31.6 us: on_device(): lax.scan(march, start, jnp.arange(depth_local, dtype=jnp.int32))]
    slice x51 -> x2, local copies, waits for them, and re-layouts: 37.5 us -> 5.32 us  [the longest x1 4.26 us: on_device(): right = lax.ppermute(volume[:, :, 0], 'col', west)]
    pallas_call x0 -> x2, Pallas kernels: none -> 16.8 us  [the longest x1 14.8 us: march(): pl.pallas_call(march_kernel, out_shape=jax.ShapeDtypeStruct((blocks, 4, S...]
  transfers between devices with their start and end apart: 6 -> 4, of which waited for: 4 -> 2; matrix products, arithmetic and copies ran while one was open for 0% -> 2% of each run, Pallas kernels for 0% -> 0%
where the time goes in v1:
time: 85.6 us; the launch traced here: 84.5 us
  blocking collectives  38.2 us (45%)
  Pallas kernels  16.8 us (20%)
  starting transfers between devices  10.8 us (13%)
  local copies, waits for them, and re-layouts  10.7 us (12%)
  waiting for transfers between devices  7.8 us (9%)
    all_to_all x1, blocking collectives, on_device(): parts = lax.all_to_all(parts, 'depth', 0, 0, tiled=True)  38.2 us
    pallas_call x1, Pallas kernels, march(): pl.pallas_call(march_kernel, out_shape=jax.ShapeDtypeStruct((blocks, 4, S...  14.8 us
    unnamed x14, local copies, waits for them, and re-layouts  5.02 us
    ppermute x1, waiting for transfers between devices, on_device(): high = lax.ppermute(volume[:1], 'depth', down)  4.3 us
    slice x1, local copies, waits for them, and re-layouts, on_device(): right = lax.ppermute(volume[:, :, 0], 'col', west)  4.26 us
    ppermute x1, starting transfers between devices, on_device(): low = lax.ppermute(volume[depth - 1:], 'depth', up)  3.84 us
    ppermute x1, starting transfers between devices, on_device(): right = lax.ppermute(volume[:, :, 0], 'col', west)  3.64 us
    ppermute x1, waiting for transfers between devices, on_device(): low = lax.ppermute(volume[depth - 1:], 'depth', up)  3.49 us
  transfers between devices with their start and end apart: 4, of which 2 were waited for; matrix products, arithmetic and copies ran while one was open for 2% of the time, Pallas kernels for 0%

profile of v1, /device:TPU:4, one launch (start us, length us, event | category | flops | bytes accessed | tf_op | source)
XLA Modules:
  0.0 84.5 jit_solution(16341059113810631386)
XLA Ops:
  0.0 4.3 %fusion = (f32[16,256,1]{2,1,0:T(8,128)S(1)}, f32[16,256,1]{2,1,0:T(8,128)}) fusion(f32[16,256,256]{2,1,0:T(8,128)} %vol.1), kind=kLoop, calls=%fused_computation.3 | loop fusion | bytes 65536 | tf_op jit(solution)/shard_map/slice | solution.py:154
  4.3 2.2 %copy.13 = f32[16,256,1]{1,0,2:T(8,128)S(1)} copy(f32[16,256,1]{2,1,0:T(8,128)} %get-tuple-element.6) | data formatting | bytes 32768
  6.5 0.0 copy-start.3
  6.5 0.0 copy-start.4
  6.5 0.0 copy-start.5
  6.5 0.0 copy-start.1
  6.5 0.0 copy-start.2
  6.5 2.1 %collective-permute-start.2 = (f32[16,256]{1,0:T(8,128)S(1)}, f32[16,256]{1,0:T(8,128)S(1)}, u32[]{:S(2)}, u32[]{:S(2)}) collective-permute-start(f32[16,256]{1,0:T(8,128)S(1)} %bitcast.11), channel_id=1, source_target_pairs={{0,1},{1,2},{2,3},{3,4},{4,5},{5,6},{6,7},{8,9},{9,10},{10,11},{11... | collective-permute-start | bytes 49160 | tf_op jit(solution)/shard_map/ppermute | solution.py:153
  8.6 0.6 copy.14
  9.2 3.6 %collective-permute-start.3 = (f32[16,256]{1,0:T(8,128)S(1)}, f32[16,256]{1,0:T(8,128)S(1)}, u32[]{:S(2)}, u32[]{:S(2)}) collective-permute-start(f32[16,256]{1,0:T(8,128)S(1)} %bitcast.10), channel_id=1, source_target_pairs={{1,0},{2,1},{3,2},{4,3},{5,4},{6,5},{7,6},{9,8},{10,9},{11,10},{12... | collective-permute-start | bytes 49160 | tf_op jit(solution)/shard_map/ppermute | solution.py:154
  12.8 1.1 %fusion.1 = (f32[1,256,256]{2,1,0:T(8,128)S(1)}, f32[1,256,256]{2,1,0:T(8,128)S(1)}) fusion(f32[16,256,256]{2,1,0:T(8,128)} %vol.1), kind=kLoop, calls=%fused_computation.4 | loop fusion | bytes 1048576 | tf_op jit(solution)/shard_map/slice | solution.py:149
  13.9 3.8 %collective-permute-start = (f32[1,256,256]{2,1,0:T(8,128)S(1)}, f32[1,256,256]{2,1,0:T(8,128)S(1)}, u32[]{:S(2)}, u32[]{:S(2)}) collective-permute-start(f32[1,256,256]{2,1,0:T(8,128)S(1)} %get-tuple-element.8), channel_id=1, source_target_pairs={{0,8},{8,16},{16,24},{24,32},{32,40},{40,48},{48,56},{56,64},{64,7... | collective-permute-start | bytes 786440 | tf_op jit(solution)/shard_map/ppermute | solution.py:148
  17.7 1.3 %collective-permute-start.1 = (f32[1,256,256]{2,1,0:T(8,128)S(1)}, f32[1,256,256]{2,1,0:T(8,128)S(1)}, u32[]{:S(2)}, u32[]{:S(2)}) collective-permute-start(f32[1,256,256]{2,1,0:T(8,128)S(1)} %get-tuple-element.7), channel_id=1, source_target_pairs={{8,0},{16,8},{24,16},{32,24},{40,32},{48,40},{56,48},{64,56},{72,6... | collective-permute-start | bytes 786440 | tf_op jit(solution)/shard_map/ppermute | solution.py:149
  19.0 0.0 copy-done.3
  19.0 0.0 copy-done.4
  19.1 0.0 copy-done.5
  19.1 0.0 copy-done.1
  19.1 0.1 reshape.9
  19.2 0.0 copy-done.2
  19.2 0.1 concatenate.3.par
  19.3 0.0 collective-permute-done.2
  19.3 0.1 copy.10
  19.4 0.0 collective-permute-done.3
  19.4 0.1 copy.12
  19.5 3.5 %collective-permute-done.low = f32[1,256,256]{2,1,0:T(8,128)S(1)} collective-permute-done((f32[1,256,256]{2,1,0:T(8,128)S(1)}, f32[1,256,256]{2,1,0:T(8,128)S(1)}, u32[]{:S(2)}, u32[]{:S(2)}) %collective-permute-start) | collective-permute-done | bytes 262176 | tf_op jit(solution)/shard_map/ppermute | solution.py:148
  23.0 4.3 %collective-permute-done.1.high = f32[1,256,256]{2,1,0:T(8,128)S(1)} collective-permute-done((f32[1,256,256]{2,1,0:T(8,128)S(1)}, f32[1,256,256]{2,1,0:T(8,128)S(1)}, u32[]{:S(2)}, u32[]{:S(2)}) %collective-permute-start.1) | collective-permute-done | bytes 262176 | tf_op jit(solution)/shard_map/ppermute | solution.py:149
  27.3 0.0 copy-start
  27.3 2.2 %copy-done = f32[16,256,256]{2,1,0:T(8,128)S(1)} copy-done((f32[16,256,256]{2,1,0:T(8,128)S(1)}, f32[16,256,256]{2,1,0:T(8,128)}, u32[]{:S(2)}) %copy-start) | copy-done | bytes 4194328
  29.5 14.8 %march.1 = f32[32,4,8,256]{3,2,1,0:T(8,128)S(1)} custom-call(f32[56]{0:T(128)S(1)} %concatenate.3.par, f32[16,256,256]{2,1,0:T(8,128)S(1)} %copy-done, f32[1,256,256]{2,1,0:T(8,128)S(1)} %collective-permute-done.low, f32[1,256,256]{2,1,0:T(8,128)S(1)} %collective-permute-done.1.high, f32[32,8,128]{2,1,0:T(8,128)S(1)} %pad.7.left, f32[32,8,128]{2,1,0:T(8,128)S(1)} %pad.8.right), custom_call_target="tpu_custom_call" | custom-call | tf_op jit(solution)/shard_map/march/pallas_call | solution.py:97
  44.3 38.2 %all_to_all.5.parts = f32[32,4,8,256]{3,2,1,0:T(8,128)} all-to-all(f32[32,4,8,256]{3,2,1,0:T(8,128)S(1)} %march.1), channel_id=1, replica_groups=mesh['depth'=32,'col'=8] {'depth'}, dimensions={0} | all-to-all | bytes 2097152 | tf_op jit(solution)/shard_map/all_to_all | solution.py:166
  82.6 1.9 %merge.1 = f32[4,8,256]{2,1,0:T(8,128)} custom-call(f32[32,4,8,256]{3,2,1,0:T(8,128)} %all_to_all.5.parts), custom_call_target="tpu_custom_call" | custom-call | tf_op jit(solution)/shard_map/merge/pallas_call | solution.py:127
  (5 shorter events, 0.0 us)
Async XLA Ops:
  6.5 12.6 %copy-start.3 = (f32[8]{0:T(128)S(1)}, f32[8]{0:T(128)}, u32[]{:S(2)}) copy-start(f32[8]{0:T(128)} %param.8) | copy-start | bytes 100
  6.5 12.6 %copy-start.4 = (f32[8]{0:T(128)S(1)}, f32[8]{0:T(128)}, u32[]{:S(2)}) copy-start(f32[8]{0:T(128)} %param.9) | copy-start | bytes 100
  6.5 12.6 %copy-start.5 = (f32[3]{0:T(128)S(1)}, f32[3]{0:T(128)}, u32[]{:S(2)}) copy-start(f32[3]{0:T(128)} %param.11) | copy-start | bytes 40
  6.5 12.6 %copy-start.1 = (f32[3,8]{1,0:T(4,128)S(1)}, f32[3,8]{1,0:T(4,128)}, u32[]{:S(2)}) copy-start(f32[3,8]{1,0:T(4,128)} %param.10) | copy-start | bytes 292
  6.5 12.7 %copy-start.2 = (f32[8]{0:T(128)S(1)}, f32[8]{0:T(128)}, u32[]{:S(2)}) copy-start(f32[8]{0:T(128)} %param.7) | copy-start | bytes 100
  6.5 12.8 %collective-permute-start.2 = (f32[16,256]{1,0:T(8,128)S(1)}, f32[16,256]{1,0:T(8,128)S(1)}, u32[]{:S(2)}, u32[]{:S(2)}) collective-permute-start(f32[16,256]{1,0:T(8,128)S(1)} %bitcast.11), channel_id=1, source_target_pairs={{0,1},{1,2},{2,3},{3,4},{4,5},{5,6},{6,7},{8,9},{9,10},{10,11},{11... | collective-permute-start | bytes 49160 | tf_op jit(solution)/shard_map/ppermute | solution.py:153
  9.2 10.2 %collective-permute-start.3 = (f32[16,256]{1,0:T(8,128)S(1)}, f32[16,256]{1,0:T(8,128)S(1)}, u32[]{:S(2)}, u32[]{:S(2)}) collective-permute-start(f32[16,256]{1,0:T(8,128)S(1)} %bitcast.10), channel_id=1, source_target_pairs={{1,0},{2,1},{3,2},{4,3},{5,4},{6,5},{7,6},{9,8},{10,9},{11,10},{12... | collective-permute-start | bytes 49160 | tf_op jit(solution)/shard_map/ppermute | solution.py:154
  13.9 9.1 %collective-permute-start = (f32[1,256,256]{2,1,0:T(8,128)S(1)}, f32[1,256,256]{2,1,0:T(8,128)S(1)}, u32[]{:S(2)}, u32[]{:S(2)}) collective-permute-start(f32[1,256,256]{2,1,0:T(8,128)S(1)} %get-tuple-element.8), channel_id=1, source_target_pairs={{0,8},{8,16},{16,24},{24,32},{32,40},{40,48},{48,56},{56,64},{64,7... | collective-permute-start | bytes 786440 | tf_op jit(solution)/shard_map/ppermute | solution.py:148
  17.7 9.6 %collective-permute-start.1 = (f32[1,256,256]{2,1,0:T(8,128)S(1)}, f32[1,256,256]{2,1,0:T(8,128)S(1)}, u32[]{:S(2)}, u32[]{:S(2)}) collective-permute-start(f32[1,256,256]{2,1,0:T(8,128)S(1)} %get-tuple-element.7), channel_id=1, source_target_pairs={{8,0},{16,8},{24,16},{32,24},{40,32},{48,40},{56,48},{64,56},{72,6... | collective-permute-start | bytes 786440 | tf_op jit(solution)/shard_map/ppermute | solution.py:149
  27.3 2.2 %copy-start = (f32[16,256,256]{2,1,0:T(8,128)S(1)}, f32[16,256,256]{2,1,0:T(8,128)}, u32[]{:S(2)}) copy-start(f32[16,256,256]{2,1,0:T(8,128)} %vol.1) | copy-start | bytes 12582916

commit v2 on v1

v2 whole, which is shorter than its diff:
```python
import functools
import math

import jax
import jax.numpy as jnp
from jax import lax
from jax.experimental import pallas as pl
from jax.experimental.pallas import tpu as pltpu
from jax.sharding import PartitionSpec as P

LANES = 128
SUB = 8
BUMPS = 8
LIMIT = 16 * 1024 * 1024
VMEM = pl.BlockSpec(memory_space=pltpu.VMEM)


def split_depth(slabs):
    zs = 8 if slabs == 32 else max(1, slabs // 2)
    return slabs // zs, zs


def prepare_kernel(
    depth_all, vol, first_slab, last_slab, center, width, density, color, light,
    cells, west, east, par, center_here, width_here, density_here, color_here, light_here, sems,
):
    del first_slab, last_slab
    depth, rows, cols = vol.shape
    tiles = cols // LANES
    copies = [
        pltpu.make_async_copy(
            vol.at[:, :, pl.ds(t * LANES, LANES)], cells.at[t, :, pl.ds(SUB, rows)], sems.at[t]
        )
        for t in range(tiles)
    ]
    small = [
        pltpu.make_async_copy(src, dst, sems.at[tiles + i])
        for i, (src, dst) in enumerate((
            (center, center_here), (width, width_here), (density, density_here),
            (color, color_here), (light, light_here),
        ))
    ]
    for copy in small + copies:
        copy.start()
    log2e = math.log2(math.e)

    def spread(ref, row, k):
        return jnp.broadcast_to(ref[pl.ds(row, 1), pl.ds(k, 1)], (SUB, LANES))

    border = jnp.zeros((tiles, depth, SUB, LANES), jnp.float32)
    cells[:, :, pl.ds(0, SUB), :] = border
    cells[:, :, pl.ds(SUB + rows, SUB), :] = border
    for copy in small:
        copy.wait()
    for k in range(BUMPS):
        scale = spread(width_here, 0, k)
        par[k] = spread(center_here, 0, k)
        par[BUMPS + k] = -log2e / (scale * scale)
        par[2 * BUMPS + k] = spread(density_here, 0, k) * (-log2e / depth_all)
        for c in range(3):
            par[32 + c * BUMPS + k] = spread(color_here, c, k)
    for a in range(3):
        par[24 + a] = spread(light_here, 0, a) * 0.7
    lane = lax.broadcasted_iota(jnp.int32, (SUB, LANES), 1)
    groups = west.shape[0]
    per_group = (rows // SUB) // groups

    def extract(t, source, out):
        def group(g, unused):
            packed = jnp.zeros((SUB, LANES), jnp.float32)
            for r in range(per_group):
                base = pl.multiple_of((g * per_group + r + 1) * SUB, SUB)
                for z in range(depth):
                    place = r * depth + z
                    tile = cells[t, z, pl.ds(base, SUB), :]
                    shift = (place - source) % LANES
                    moved = pltpu.roll(tile, shift, 1) if shift else tile
                    packed = jnp.where(lane == place, moved, packed)
            out[g] = packed
            return 0

        lax.fori_loop(0, groups, group, 0)

    copies[0].wait()
    extract(0, 0, west)
    for copy in copies[1:]:
        copy.wait()
    extract(tiles - 1, LANES - 1, east)


def prepare(depth_all, vol, *small):
    depth, rows, cols = vol.shape
    groups = -(-(rows // SUB) * depth // LANES)
    edge = jax.ShapeDtypeStruct((groups, SUB, LANES), jnp.float32)
    return pl.pallas_call(
        functools.partial(prepare_kernel, depth_all),
        out_shape=(
            jax.ShapeDtypeStruct((cols // LANES, depth, rows + 2 * SUB, LANES), jnp.float32),
            edge,
            edge,
            jax.ShapeDtypeStruct((32 + 3 * BUMPS, SUB, LANES), jnp.float32),
        ),
        in_specs=[pl.BlockSpec(memory_space=pl.ANY)] * 8,
        out_specs=(VMEM, VMEM, VMEM, VMEM),
        scratch_shapes=[pltpu.VMEM(x.shape, jnp.float32) for x in small[-5:]]
        + [pltpu.SemaphoreType.DMA((cols // LANES + 5,))],
        compiler_params=pltpu.CompilerParams(vmem_limit_bytes=LIMIT),
        name="prepare",
    )(vol, *small)


def march_kernel(shifts, ys, zs, par, cells, low, high, left, right, *outs):
    tiles, depth = cells.shape[:2]
    here_z = lax.rem(lax.axis_index("depth"), zs)
    lane = lax.broadcasted_iota(jnp.int32, (SUB, LANES), 1)
    first = lane == 0
    last = lane == LANES - 1
    per_group = LANES // depth

    def block(i, unused):
        which, j = lax.div(i, ys), lax.rem(i, ys)
        shift = shifts[0]
        for q in range(1, len(shifts)):
            shift = jnp.where(which == q, shifts[q], shift)
        rb = j * zs + lax.rem(here_z + shift, zs)
        row = pl.multiple_of(rb * SUB, SUB)
        base = pl.multiple_of(rb * SUB + SUB, SUB)

        def cell(t, z, move=0):
            if z < 0 or z >= depth:
                side = low if z < 0 else high
                return side[pl.ds(row, SUB), pl.ds(t * LANES, LANES)]
            return cells[t, z, pl.ds(base + move, SUB), :]

        group = lax.div(rb, per_group)
        turn = lax.rem(LANES - lax.rem(rb, per_group) * depth, LANES)
        halo_left = pltpu.roll(left[group], turn, 1)
        halo_right = pltpu.roll(right[group], turn, 1)
        acc = [[None] * BUMPS for t in range(tiles)]
        logt = [None] * tiles
        trans = [None] * tiles
        for z in range(depth):
            here = [cell(t, z) for t in range(tiles)]
            fwd = [pltpu.roll(h, 1, 1) for h in here]
            bwd = [pltpu.roll(h, LANES - 1, 1) for h in here]
            lo = halo_left if z == 0 else pltpu.roll(halo_left, LANES - z, 1)
            hi = pltpu.roll(halo_right, LANES - 1 - z, 1)
            for t in range(tiles):
                v = here[t]
                from_left = jnp.where(first, lo if t == 0 else fwd[t - 1], fwd[t])
                from_right = jnp.where(last, hi if t == tiles - 1 else bwd[t + 1], bwd[t])
                dx = from_right - from_left
                dy = cell(t, z, 1) - cell(t, z, -1)
                dz = cell(t, z + 1) - cell(t, z - 1)
                lit = jnp.abs(par[24] * dx + par[25] * dy + par[26] * dz)
                norm = (dx * dx + dy * dy) + (dz * dz + 4.0)
                shade = 0.3 + lit * lax.rsqrt(norm)
                b = []
                for k in range(BUMPS):
                    u = v - par[k]
                    b.append(jnp.exp2(u * u * par[8 + k]))
                e = [b[k] * par[16 + k] for k in range(BUMPS)]
                ext = ((e[0] + e[1]) + (e[2] + e[3])) + ((e[4] + e[5]) + (e[6] + e[7]))
                logt[t] = ext if z == 0 else logt[t] + ext
                after = jnp.exp2(logt[t])
                weight = ((1.0 if z == 0 else trans[t]) - after) * shade
                trans[t] = after
                for k in range(BUMPS):
                    term = weight * b[k]
                    acc[t][k] = term if z == 0 else acc[t][k] + term
        totals = []
        for t in range(tiles):
            for c in range(3):
                total = acc[t][0] * par[32 + c * BUMPS]
                for k in range(1, BUMPS):
                    total = total + acc[t][k] * par[32 + c * BUMPS + k]
                totals.append((t, c, total))
            totals.append((t, 3, logt[t]))
        for q, out in enumerate(outs):
            @pl.when(which == q)
            def store():
                for t, c, total in totals:
                    out[j, c, :, pl.ds(t * LANES, LANES)] = total
        return 0

    lax.fori_loop(0, len(shifts) * ys, block, 0)


def march(shifts, ys, zs, par, cells, low, high, left, right):
    tiles, depth = cells.shape[:2]
    work = len(shifts) * ys * SUB * tiles * LANES * depth
    return pl.pallas_call(
        functools.partial(march_kernel, shifts, ys, zs),
        out_shape=[jax.ShapeDtypeStruct((ys, 4, SUB, tiles * LANES), jnp.float32)] * len(shifts),
        in_specs=[VMEM] * 6,
        out_specs=[VMEM] * len(shifts),
        compiler_params=pltpu.CompilerParams(vmem_limit_bytes=LIMIT),
        cost_estimate=pl.CostEstimate(
            flops=80 * work, bytes_accessed=4 * work, transcendentals=10 * work
        ),
        name="march%d" % shifts[0],
    )(par, cells, low, high, left, right)


def over(parts, here):
    color, logt = [jnp.zeros_like(parts[0][0])] * 3, jnp.zeros_like(parts[0][3])
    back, back_logt = color, logt
    for s in reversed(range(len(parts))):
        turn = here == s
        back = [jnp.where(turn, a, b) for a, b in zip(color, back)]
        back_logt = jnp.where(turn, logt, back_logt)
        color = [jnp.where(turn, 0.0, a) for a in color]
        logt = jnp.where(turn, 0.0, logt)
        seen = jnp.exp2(logt)
        color = [a + seen * parts[s][c] for c, a in enumerate(color)]
        logt = logt + parts[s][3]
    seen = jnp.exp2(logt)
    return [a + seen * b for a, b in zip(color, back)], logt + back_logt


def merge_z_kernel(ys, zs, *refs):
    parts, outs = refs[:zs], refs[zs:]
    me = lax.axis_index("depth")
    y, z = lax.div(me, zs), lax.rem(me, zs)
    for t in range(ys):
        j = lax.rem(y + t, ys)
        color, logt = over([[p[j, c] for c in range(4)] for p in parts], z)
        for c in range(3):
            outs[t][c] = color[c]
        outs[t][3] = logt


def merge_z(ys, zs, parts):
    shape = parts[0].shape[1:]
    return pl.pallas_call(
        functools.partial(merge_z_kernel, ys, zs),
        out_shape=[jax.ShapeDtypeStruct(shape, jnp.float32)] * ys,
        in_specs=[VMEM] * zs,
        out_specs=[VMEM] * ys,
        compiler_params=pltpu.CompilerParams(vmem_limit_bytes=LIMIT),
        name="merge_z",
    )(*parts)


def merge_y_kernel(zs, *refs):
    parts, out = refs[:-1], refs[-1]
    y = lax.div(lax.axis_index("depth"), zs)
    color, logt = over([[p[c] for c in range(4)] for p in parts], y)
    for c in range(3):
        out[c] = color[c]
    out[3] = 1.0 - jnp.exp2(logt)


def merge_y(zs, parts):
    return pl.pallas_call(
        functools.partial(merge_y_kernel, zs),
        out_shape=jax.ShapeDtypeStruct(parts[0].shape, jnp.float32),
        in_specs=[VMEM] * len(parts),
        out_specs=VMEM,
        compiler_params=pltpu.CompilerParams(vmem_limit_bytes=LIMIT),
        name="merge_y",
    )(*parts)


def in_hbm(x):
    return pltpu.with_memory_space_constraint(x, pltpu.HBM)


def on_device(volume, tf_center, tf_width, tf_density, tf_color, light):
    depth, rows, cols = volume.shape
    slabs = lax.axis_size("depth")
    ys, zs = split_depth(slabs)
    depth_all = depth * slabs
    up = [(i, i + 1) for i in range(slabs - 1)]
    down = [(j, i) for i, j in up]
    first_slab, last_slab = volume[0], volume[depth - 1]
    low = lax.ppermute(last_slab, "depth", up)
    high = lax.ppermute(first_slab, "depth", down)
    cells, west_edge, east_edge, par = prepare(
        depth_all, in_hbm(volume), first_slab, last_slab, in_hbm(tf_center[None]),
        in_hbm(tf_width[None]), in_hbm(tf_density[None]), in_hbm(tf_color), in_hbm(light[None]),
    )
    width = lax.axis_size("col")
    east = [(i, i + 1) for i in range(width - 1)]
    west = [(j, i) for i, j in east]
    left = lax.ppermute(east_edge, "col", east)
    right = lax.ppermute(west_edge, "col", west)

    order = sorted(range(zs), key=lambda s: -min(s, zs - s))
    arrived = [None] * zs
    cuts = [0, 1, 3, 5, 8] if zs == 8 else [0, zs]
    for begin, end in zip(cuts, cuts[1:]):
        shifts = order[begin:end]
        parts = march(shifts, ys, zs, par, cells, low, high, left, right)
        for s, part in zip(shifts, parts):
            if s:
                pairs = [(y * zs + z, y * zs + (z + s) % zs) for y in range(ys) for z in range(zs)]
                part = lax.ppermute(part, "depth", pairs)
            arrived[s] = part
    merged = list(merge_z(ys, zs, arrived))
    for t in range(1, ys):
        pairs = [(i, (i + t * zs) % slabs) for i in range(slabs)]
        merged[t] = lax.ppermute(merged[t], "depth", pairs)
    return merge_y(zs, merged)


def solution(mesh):
    return jax.shard_map(
        on_device,
        mesh=mesh,
        in_specs=(P("depth", None, "col"), P(), P(), P(), P(), P()),
        out_specs=P(None, "depth", "col"),
        check_vma=False,
    )
```

time: 85.6 us -> 67.3 us (0.79)
  blocking collectives: 38.2 us -> 0 us
  starting transfers between devices: 10.8 us -> 38.4 us
  local copies, waits for them, and re-layouts: 10.7 us -> 1.06 us
  Pallas kernels: 16.8 us -> 20 us
    all_to_all x1 -> x0, blocking collectives: 38.2 us -> none  [on_device(): parts = lax.all_to_all(parts, 'depth', 0, 0, tiled=True)]
    ppermute x4 -> x14, starting transfers between devices: 10.8 us -> 38.4 us  [the longest x7 21.8 us: on_device(): part = lax.ppermute(part, 'depth', pairs)]
    slice x2 -> x0, local copies, waits for them, and re-layouts: 5.32 us -> none  [the longest x1 4.26 us: on_device(): right = lax.ppermute(volume[:, :, 0], 'col', west)]
    unnamed x14 -> x0, local copies, waits for them, and re-layouts: 5.02 us -> none
    pallas_call x2 -> x7, Pallas kernels: 16.8 us -> 20 us  [the longest x4 15.8 us: march(): pl.pallas_call(functools.partial(march_kernel, shifts, ys, zs), out_shape...]
    squeeze x0 -> x1, local copies, waits for them, and re-layouts: none -> 1.06 us  [on_device(): first_slab, last_slab = (volume[0], volume[depth - 1])]
    ppermute x4 -> x14, waiting for transfers between devices: 7.8 us -> 7.25 us  [the longest x7 3.27 us: on_device(): part = lax.ppermute(part, 'depth', pairs)]
  transfers between devices with their start and end apart: 4 -> 14, of which waited for: 2 -> 4; matrix products, arithmetic and copies ran while one was open for 2% -> 0% of each run, Pallas kernels for 0% -> 26%
where the time goes in v2:
time: 67.3 us; the launch traced here: 66.8 us
  starting transfers between devices  38.4 us (57%)
  Pallas kernels  20 us (30%)
  waiting for transfers between devices  7.25 us (11%)
  local copies, waits for them, and re-layouts  1.06 us (2%)
    ppermute x7, starting transfers between devices, on_device(): part = lax.ppermute(part, 'depth', pairs)  21.8 us
    pallas_call x4, Pallas kernels, march(): pl.pallas_call(functools.partial(march_kernel, shifts, ys, zs), out_shape...  15.8 us
    ppermute x3, starting transfers between devices, on_device(): merged[t] = lax.ppermute(merged[t], 'depth', pairs)  5.9 us
    ppermute x1, starting transfers between devices, on_device(): low = lax.ppermute(last_slab, 'depth', up)  3.84 us
    ppermute x1, starting transfers between devices, on_device(): right = lax.ppermute(west_edge, 'col', west)  3.64 us
    pallas_call x1, Pallas kernels, prepare(): pl.pallas_call(functools.partial(prepare_kernel, depth_all), out_shape=(j...  3.4 us
    ppermute x7, waiting for transfers between devices, on_device(): part = lax.ppermute(part, 'depth', pairs)  3.27 us
    ppermute x3, waiting for transfers between devices, on_device(): merged[t] = lax.ppermute(merged[t], 'depth', pairs)  2.56 us
  transfers between devices with their start and end apart: 14, of which 4 were waited for; matrix products, arithmetic and copies ran while one was open for 0% of the time, Pallas kernels for 26%

profile of v2, /device:TPU:4, one launch (start us, length us, event | category | flops | bytes accessed | tf_op | source)
XLA Modules:
  0.0 66.8 jit_solution(8275766582530423444)
XLA Ops:
  0.0 1.1 %slice_bitcast_fusion = (f32[256,256]{1,0:T(8,128)S(1)}, f32[256,256]{1,0:T(8,128)S(1)}) fusion(f32[16,256,256]{2,1,0:T(8,128)} %vol.1), kind=kLoop, calls=%fused_computation | loop fusion | bytes 1048576 | tf_op jit(solution)/shard_map/squeeze | solution.py:276
  1.1 3.8 %collective-permute-start = (f32[256,256]{1,0:T(8,128)S(1)}, f32[256,256]{1,0:T(8,128)S(1)}, u32[]{:S(2)}, u32[]{:S(2)}) collective-permute-start(f32[256,256]{1,0:T(8,128)S(1)} %get-tuple-element.35.last_slab), channel_id=1, source_target_pairs={{0,8},{8,16},{16,24},{24,32},{32,40},{40,48},{48,56},{56,64},{64,7... | collective-permute-start | bytes 786440 | tf_op jit(solution)/shard_map/ppermute | solution.py:277
  4.9 1.3 %collective-permute-start.1 = (f32[256,256]{1,0:T(8,128)S(1)}, f32[256,256]{1,0:T(8,128)S(1)}, u32[]{:S(2)}, u32[]{:S(2)}) collective-permute-start(f32[256,256]{1,0:T(8,128)S(1)} %get-tuple-element.36.first_slab), channel_id=1, source_target_pairs={{8,0},{16,8},{24,16},{32,24},{40,32},{48,40},{56,48},{64,56},{72,6... | collective-permute-start | bytes 786440 | tf_op jit(solution)/shard_map/ppermute | solution.py:278
  6.2 3.4 %prepare.1 = (f32[2,16,272,128]{3,2,1,0:T(8,128)S(1)}, f32[4,8,128]{2,1,0:T(8,128)S(1)}, f32[4,8,128]{2,1,0:T(8,128)S(1)}, f32[56,8,128]{2,1,0:T(8,128)S(1)}) custom-call(f32[16,256,256]{2,1,0:T(8,128)} %vol.1, f32[256,256]{1,0:T(8,128)S(1)} %get-tuple-element.36.first_slab, f32[256,256]{1,0:T(8,128)S(1)} %get-tuple-element.35.last_slab, f32[1,8]{1,0:T(1,128)} %bitcast.8, ...), custom_call_target="tpu_custom_call" | custom-call | tf_op jit(solution)/shard_map/prepare/pallas_call | solution.py:95
  9.6 1.9 %collective-permute-start.2 = (f32[4,8,128]{2,1,0:T(8,128)S(1)}, f32[4,8,128]{2,1,0:T(8,128)S(1)}, u32[]{:S(2)}, u32[]{:S(2)}) collective-permute-start(f32[4,8,128]{2,1,0:T(8,128)S(1)} %get-tuple-element.22), channel_id=1, source_target_pairs={{0,1},{1,2},{2,3},{3,4},{4,5},{5,6},{6,7},{8,9},{9,10},{10,11},{11... | collective-permute-start | bytes 49160 | tf_op jit(solution)/shard_map/ppermute | solution.py:286
  11.5 3.6 %collective-permute-start.3 = (f32[4,8,128]{2,1,0:T(8,128)S(1)}, f32[4,8,128]{2,1,0:T(8,128)S(1)}, u32[]{:S(2)}, u32[]{:S(2)}) collective-permute-start(f32[4,8,128]{2,1,0:T(8,128)S(1)} %get-tuple-element.23), channel_id=1, source_target_pairs={{1,0},{2,1},{3,2},{4,3},{5,4},{6,5},{7,6},{9,8},{10,9},{11,10},{12... | collective-permute-start | bytes 49160 | tf_op jit(solution)/shard_map/ppermute | solution.py:287
  15.2 0.0 collective-permute-done.2.left
  15.2 1.4 %collective-permute-done.3.right = f32[4,8,128]{2,1,0:T(8,128)S(1)} collective-permute-done((f32[4,8,128]{2,1,0:T(8,128)S(1)}, f32[4,8,128]{2,1,0:T(8,128)S(1)}, u32[]{:S(2)}, u32[]{:S(2)}) %collective-permute-start.3) | collective-permute-done | bytes 16416 | tf_op jit(solution)/shard_map/ppermute | solution.py:287
  16.6 0.0 collective-permute-done.low
  16.6 0.0 collective-permute-done.1.high
  16.6 1.9 %march4.1 = f32[4,4,8,256]{3,2,1,0:T(8,128)S(1)} custom-call(f32[56,8,128]{2,1,0:T(8,128)S(1)} %get-tuple-element.20.par, f32[2,16,272,128]{3,2,1,0:T(8,128)S(1)} %get-tuple-element.21.cells, f32[256,256]{1,0:T(8,128)S(1)} %collective-permute-done.low, f32[256,256]{1,0:T(8,128)S(1)} %collective-permute-done.1.high, ...), custom_call_target="tpu_custom_call" | custom-call | flops 10485760 | bytes 524288 | tf_op jit(solution)/shard_map/march4/pallas_call | solution.py:192
  18.5 9.2 %collective-permute-start.7 = (f32[4,4,8,256]{3,2,1,0:T(8,128)S(1)}, f32[4,4,8,256]{3,2,1,0:T(8,128)S(1)}, u32[]{:S(2)}, u32[]{:S(2)}) collective-permute-start(f32[4,4,8,256]{3,2,1,0:T(8,128)S(1)} %march4.1), channel_id=1, source_target_pairs={{0,32},{8,40},{16,48},{24,56},{32,0},{40,8},{48,16},{56,24},{64,96... | collective-permute-start | bytes 393224 | tf_op jit(solution)/shard_map/ppermute | solution.py:298
  27.7 4.0 %march3.1 = (f32[4,4,8,256]{3,2,1,0:T(8,128)S(1)}, f32[4,4,8,256]{3,2,1,0:T(8,128)S(1)}) custom-call(f32[56,8,128]{2,1,0:T(8,128)S(1)} %get-tuple-element.20.par, f32[2,16,272,128]{3,2,1,0:T(8,128)S(1)} %get-tuple-element.21.cells, f32[256,256]{1,0:T(8,128)S(1)} %collective-permute-done.low, f32[256,256]{1,0:T(8,128)S(1)} %collective-permute-done.1.high, ...), custom_call_target="tpu_custom_call" | custom-call | flops 20971520 | bytes 1048576 | tf_op jit(solution)/shard_map/march3/pallas_call | solution.py:192
  31.7 0.8 %collective-permute-start.6 = (f32[4,4,8,256]{3,2,1,0:T(8,128)S(1)}, f32[4,4,8,256]{3,2,1,0:T(8,128)S(1)}, u32[]{:S(2)}, u32[]{:S(2)}) collective-permute-start(f32[4,4,8,256]{3,2,1,0:T(8,128)S(1)} %get-tuple-element.27), channel_id=1, source_target_pairs={{0,24},{8,32},{16,40},{24,48},{32,56},{40,0},{48,8},{56,16},{64,88... | collective-permute-start | bytes 393224 | tf_op jit(solution)/shard_map/ppermute | solution.py:298
  32.5 4.3 %collective-permute-start.8 = (f32[4,4,8,256]{3,2,1,0:T(8,128)S(1)}, f32[4,4,8,256]{3,2,1,0:T(8,128)S(1)}, u32[]{:S(2)}, u32[]{:S(2)}) collective-permute-start(f32[4,4,8,256]{3,2,1,0:T(8,128)S(1)} %get-tuple-element.28), channel_id=1, source_target_pairs={{0,40},{8,48},{16,56},{24,0},{32,8},{40,16},{48,24},{56,32},{64,10... | collective-permute-start | bytes 393224 | tf_op jit(solution)/shard_map/ppermute | solution.py:298
  36.8 4.0 %march2.1 = (f32[4,4,8,256]{3,2,1,0:T(8,128)S(1)}, f32[4,4,8,256]{3,2,1,0:T(8,128)S(1)}) custom-call(f32[56,8,128]{2,1,0:T(8,128)S(1)} %get-tuple-element.20.par, f32[2,16,272,128]{3,2,1,0:T(8,128)S(1)} %get-tuple-element.21.cells, f32[256,256]{1,0:T(8,128)S(1)} %collective-permute-done.low, f32[256,256]{1,0:T(8,128)S(1)} %collective-permute-done.1.high, ...), custom_call_target="tpu_custom_call" | custom-call | flops 20971520 | bytes 1048576 | tf_op jit(solution)/shard_map/march2/pallas_call | solution.py:192
  40.8 0.3 collective-permute-start.5
  41.1 3.9 %collective-permute-start.9 = (f32[4,4,8,256]{3,2,1,0:T(8,128)S(1)}, f32[4,4,8,256]{3,2,1,0:T(8,128)S(1)}, u32[]{:S(2)}, u32[]{:S(2)}) collective-permute-start(f32[4,4,8,256]{3,2,1,0:T(8,128)S(1)} %get-tuple-element.29), channel_id=1, source_target_pairs={{0,48},{8,56},{16,0},{24,8},{32,16},{40,24},{48,32},{56,40},{64,11... | collective-permute-start | bytes 393224 | tf_op jit(solution)/shard_map/ppermute | solution.py:298
  45.0 6.0 %march1.1 = (f32[4,4,8,256]{3,2,1,0:T(8,128)S(1)}, f32[4,4,8,256]{3,2,1,0:T(8,128)S(1)}, f32[4,4,8,256]{3,2,1,0:T(8,128)S(1)}) custom-call(f32[56,8,128]{2,1,0:T(8,128)S(1)} %get-tuple-element.20.par, f32[2,16,272,128]{3,2,1,0:T(8,128)S(1)} %get-tuple-element.21.cells, f32[256,256]{1,0:T(8,128)S(1)} %collective-permute-done.low, ...), custom_call_target="tpu_custom_call" | custom-call | flops 31457280 | bytes 1572864 | tf_op jit(solution)/shard_map/march1/pallas_call | solution.py:192
  51.0 0.1 collective-permute-start.4
  51.1 3.2 %collective-permute-start.10 = (f32[4,4,8,256]{3,2,1,0:T(8,128)S(1)}, f32[4,4,8,256]{3,2,1,0:T(8,128)S(1)}, u32[]{:S(2)}, u32[]{:S(2)}) collective-permute-start(f32[4,4,8,256]{3,2,1,0:T(8,128)S(1)} %get-tuple-element.30), channel_id=1, source_target_pairs={{0,56},{8,0},{16,8},{24,16},{32,24},{40,32},{48,40},{56,48},{64,12... | collective-permute-start | bytes 393224 | tf_op jit(solution)/shard_map/ppermute | solution.py:298
  54.3 0.0 collective-permute-done.8.refs_5_
  54.3 0.0 collective-permute-done.5.refs_2_
  54.3 0.0 collective-permute-done.9.refs_6_
  54.3 3.3 %collective-permute-done.4.refs_1_ = f32[4,4,8,256]{3,2,1,0:T(8,128)S(1)} collective-permute-done((f32[4,4,8,256]{3,2,1,0:T(8,128)S(1)}, f32[4,4,8,256]{3,2,1,0:T(8,128)S(1)}, u32[]{:S(2)}, u32[]{:S(2)}) %collective-permute-start.4) | collective-permute-done | bytes 131104 | tf_op jit(solution)/shard_map/ppermute | solution.py:298
  57.6 0.1 merge_z.1
  57.7 1.7 %collective-permute-start.11 = (f32[4,8,256]{2,1,0:T(8,128)S(1)}, f32[4,8,256]{2,1,0:T(8,128)S(1)}, u32[]{:S(2)}, u32[]{:S(2)}) collective-permute-start(f32[4,8,256]{2,1,0:T(8,128)S(1)} %get-tuple-element.32), channel_id=1, source_target_pairs={{0,64},{8,72},{16,80},{24,88},{32,96},{40,104},{48,112},{56,120},{... | collective-permute-start | bytes 98312 | tf_op jit(solution)/shard_map/ppermute | solution.py:303
  59.4 2.9 %collective-permute-start.12 = (f32[4,8,256]{2,1,0:T(8,128)S(1)}, f32[4,8,256]{2,1,0:T(8,128)S(1)}, u32[]{:S(2)}, u32[]{:S(2)}) collective-permute-start(f32[4,8,256]{2,1,0:T(8,128)S(1)} %get-tuple-element.33), channel_id=1, source_target_pairs={{0,128},{8,136},{16,144},{24,152},{32,160},{40,168},{48,176},{56,1... | collective-permute-start | bytes 98312 | tf_op jit(solution)/shard_map/ppermute | solution.py:303
  62.3 1.3 %collective-permute-start.13 = (f32[4,8,256]{2,1,0:T(8,128)S(1)}, f32[4,8,256]{2,1,0:T(8,128)S(1)}, u32[]{:S(2)}, u32[]{:S(2)}) collective-permute-start(f32[4,8,256]{2,1,0:T(8,128)S(1)} %get-tuple-element.34), channel_id=1, source_target_pairs={{0,192},{8,200},{16,208},{24,216},{32,224},{40,232},{48,240},{56,2... | collective-permute-start | bytes 98312 | tf_op jit(solution)/shard_map/ppermute | solution.py:303
  63.6 1.2 %collective-permute-done.12.refs_2_ = f32[4,8,256]{2,1,0:T(8,128)S(1)} collective-permute-done((f32[4,8,256]{2,1,0:T(8,128)S(1)}, f32[4,8,256]{2,1,0:T(8,128)S(1)}, u32[]{:S(2)}, u32[]{:S(2)}) %collective-permute-start.12) | collective-permute-done | bytes 32800 | tf_op jit(solution)/shard_map/ppermute | solution.py:303
  64.8 1.4 %collective-permute-done.13.refs_3_ = f32[4,8,256]{2,1,0:T(8,128)S(1)} collective-permute-done((f32[4,8,256]{2,1,0:T(8,128)S(1)}, f32[4,8,256]{2,1,0:T(8,128)S(1)}, u32[]{:S(2)}, u32[]{:S(2)}) %collective-permute-start.13) | collective-permute-done | bytes 32800 | tf_op jit(solution)/shard_map/ppermute | solution.py:303
  66.2 0.6 merge_y.1
  (4 shorter events, 0.0 us)
Async XLA Ops:
  1.1 15.6 %collective-permute-start = (f32[256,256]{1,0:T(8,128)S(1)}, f32[256,256]{1,0:T(8,128)S(1)}, u32[]{:S(2)}, u32[]{:S(2)}) collective-permute-start(f32[256,256]{1,0:T(8,128)S(1)} %get-tuple-element.35.last_slab), channel_id=1, source_target_pairs={{0,8},{8,16},{16,24},{24,32},{32,40},{40,48},{48,56},{56,64},{64,7... | collective-permute-start | bytes 786440 | tf_op jit(solution)/shard_map/ppermute | solution.py:277
  4.9 11.7 %collective-permute-start.1 = (f32[256,256]{1,0:T(8,128)S(1)}, f32[256,256]{1,0:T(8,128)S(1)}, u32[]{:S(2)}, u32[]{:S(2)}) collective-permute-start(f32[256,256]{1,0:T(8,128)S(1)} %get-tuple-element.36.first_slab), channel_id=1, source_target_pairs={{8,0},{16,8},{24,16},{32,24},{40,32},{48,40},{56,48},{64,56},{72,6... | collective-permute-start | bytes 786440 | tf_op jit(solution)/shard_map/ppermute | solution.py:278
  9.6 5.6 %collective-permute-start.2 = (f32[4,8,128]{2,1,0:T(8,128)S(1)}, f32[4,8,128]{2,1,0:T(8,128)S(1)}, u32[]{:S(2)}, u32[]{:S(2)}) collective-permute-start(f32[4,8,128]{2,1,0:T(8,128)S(1)} %get-tuple-element.22), channel_id=1, source_target_pairs={{0,1},{1,2},{2,3},{3,4},{4,5},{5,6},{6,7},{8,9},{9,10},{10,11},{11... | collective-permute-start | bytes 49160 | tf_op jit(solution)/shard_map/ppermute | solution.py:286
  11.5 5.1 %collective-permute-start.3 = (f32[4,8,128]{2,1,0:T(8,128)S(1)}, f32[4,8,128]{2,1,0:T(8,128)S(1)}, u32[]{:S(2)}, u32[]{:S(2)}) collective-permute-start(f32[4,8,128]{2,1,0:T(8,128)S(1)} %get-tuple-element.23), channel_id=1, source_target_pairs={{1,0},{2,1},{3,2},{4,3},{5,4},{6,5},{7,6},{9,8},{10,9},{11,10},{12... | collective-permute-start | bytes 49160 | tf_op jit(solution)/shard_map/ppermute | solution.py:287
  18.5 32.5 %collective-permute-start.7 = (f32[4,4,8,256]{3,2,1,0:T(8,128)S(1)}, f32[4,4,8,256]{3,2,1,0:T(8,128)S(1)}, u32[]{:S(2)}, u32[]{:S(2)}) collective-permute-start(f32[4,4,8,256]{3,2,1,0:T(8,128)S(1)} %march4.1), channel_id=1, source_target_pairs={{0,32},{8,40},{16,48},{24,56},{32,0},{40,8},{48,16},{56,24},{64,96... | collective-permute-start | bytes 393224 | tf_op jit(solution)/shard_map/ppermute | solution.py:298
  31.7 19.4 %collective-permute-start.6 = (f32[4,4,8,256]{3,2,1,0:T(8,128)S(1)}, f32[4,4,8,256]{3,2,1,0:T(8,128)S(1)}, u32[]{:S(2)}, u32[]{:S(2)}) collective-permute-start(f32[4,4,8,256]{3,2,1,0:T(8,128)S(1)} %get-tuple-element.27), channel_id=1, source_target_pairs={{0,24},{8,32},{16,40},{24,48},{32,56},{40,0},{48,8},{56,16},{64,88... | collective-permute-start | bytes 393224 | tf_op jit(solution)/shard_map/ppermute | solution.py:298
  32.5 21.8 %collective-permute-start.8 = (f32[4,4,8,256]{3,2,1,0:T(8,128)S(1)}, f32[4,4,8,256]{3,2,1,0:T(8,128)S(1)}, u32[]{:S(2)}, u32[]{:S(2)}) collective-permute-start(f32[4,4,8,256]{3,2,1,0:T(8,128)S(1)} %get-tuple-element.28), channel_id=1, source_target_pairs={{0,40},{8,48},{16,56},{24,0},{32,8},{40,16},{48,24},{56,32},{64,10... | collective-permute-start | bytes 393224 | tf_op jit(solution)/shard_map/ppermute | solution.py:298
  40.8 13.6 %collective-permute-start.5 = (f32[4,4,8,256]{3,2,1,0:T(8,128)S(1)}, f32[4,4,8,256]{3,2,1,0:T(8,128)S(1)}, u32[]{:S(2)}, u32[]{:S(2)}) collective-permute-start(f32[4,4,8,256]{3,2,1,0:T(8,128)S(1)} %get-tuple-element.26), channel_id=1, source_target_pairs={{0,16},{8,24},{16,32},{24,40},{32,48},{40,56},{48,0},{56,8},{64,80... | collective-permute-start | bytes 393224 | tf_op jit(solution)/shard_map/ppermute | solution.py:298
  41.1 13.3 %collective-permute-start.9 = (f32[4,4,8,256]{3,2,1,0:T(8,128)S(1)}, f32[4,4,8,256]{3,2,1,0:T(8,128)S(1)}, u32[]{:S(2)}, u32[]{:S(2)}) collective-permute-start(f32[4,4,8,256]{3,2,1,0:T(8,128)S(1)} %get-tuple-element.29), channel_id=1, source_target_pairs={{0,48},{8,56},{16,0},{24,8},{32,16},{40,24},{48,32},{56,40},{64,11... | collective-permute-start | bytes 393224 | tf_op jit(solution)/shard_map/ppermute | solution.py:298
  51.0 6.6 %collective-permute-start.4 = (f32[4,4,8,256]{3,2,1,0:T(8,128)S(1)}, f32[4,4,8,256]{3,2,1,0:T(8,128)S(1)}, u32[]{:S(2)}, u32[]{:S(2)}) collective-permute-start(f32[4,4,8,256]{3,2,1,0:T(8,128)S(1)} %get-tuple-element.25), channel_id=1, source_target_pairs={{0,8},{8,16},{16,24},{24,32},{32,40},{40,48},{48,56},{56,0},{64,72... | collective-permute-start | bytes 393224 | tf_op jit(solution)/shard_map/ppermute | solution.py:298
  51.1 6.5 %collective-permute-start.10 = (f32[4,4,8,256]{3,2,1,0:T(8,128)S(1)}, f32[4,4,8,256]{3,2,1,0:T(8,128)S(1)}, u32[]{:S(2)}, u32[]{:S(2)}) collective-permute-start(f32[4,4,8,256]{3,2,1,0:T(8,128)S(1)} %get-tuple-element.30), channel_id=1, source_target_pairs={{0,56},{8,0},{16,8},{24,16},{32,24},{40,32},{48,40},{56,48},{64,12... | collective-permute-start | bytes 393224 | tf_op jit(solution)/shard_map/ppermute | solution.py:298
  57.7 5.9 %collective-permute-start.11 = (f32[4,8,256]{2,1,0:T(8,128)S(1)}, f32[4,8,256]{2,1,0:T(8,128)S(1)}, u32[]{:S(2)}, u32[]{:S(2)}) collective-permute-start(f32[4,8,256]{2,1,0:T(8,128)S(1)} %get-tuple-element.32), channel_id=1, source_target_pairs={{0,64},{8,72},{16,80},{24,88},{32,96},{40,104},{48,112},{56,120},{... | collective-permute-start | bytes 98312 | tf_op jit(solution)/shard_map/ppermute | solution.py:303
  59.4 5.4 %collective-permute-start.12 = (f32[4,8,256]{2,1,0:T(8,128)S(1)}, f32[4,8,256]{2,1,0:T(8,128)S(1)}, u32[]{:S(2)}, u32[]{:S(2)}) collective-permute-start(f32[4,8,256]{2,1,0:T(8,128)S(1)} %get-tuple-element.33), channel_id=1, source_target_pairs={{0,128},{8,136},{16,144},{24,152},{32,160},{40,168},{48,176},{56,1... | collective-permute-start | bytes 98312 | tf_op jit(solution)/shard_map/ppermute | solution.py:303
  62.3 3.9 %collective-permute-start.13 = (f32[4,8,256]{2,1,0:T(8,128)S(1)}, f32[4,8,256]{2,1,0:T(8,128)S(1)}, u32[]{:S(2)}, u32[]{:S(2)}) collective-permute-start(f32[4,8,256]{2,1,0:T(8,128)S(1)} %get-tuple-element.34), channel_id=1, source_target_pairs={{0,192},{8,200},{16,208},{24,216},{32,224},{40,232},{48,240},{56,2... | collective-permute-start | bytes 98312 | tf_op jit(solution)/shard_map/ppermute | solution.py:303

commit v3 on v2

v3 whole, which is shorter than its diff:
```python
import functools
import math

import jax
import jax.numpy as jnp
from jax import lax
from jax.experimental import pallas as pl
from jax.experimental.pallas import tpu as pltpu
from jax.sharding import PartitionSpec as P

LANES = 128
SUB = 8
BUMPS = 8
LIMIT = 16 * 1024 * 1024
MIX = 256
BODY = 2
VMEM = pl.BlockSpec(memory_space=pltpu.VMEM)


def split_depth(slabs):
    zs = 8 if slabs == 32 else max(1, slabs // 2)
    return slabs // zs, zs


def thirds(x):
    one = x.astype(jnp.bfloat16).astype(jnp.float32)
    rest = x - one
    two = rest.astype(jnp.bfloat16).astype(jnp.float32)
    return one, two, rest - two


def prepare_kernel(
    depth_all, vol, first_slab, last_slab, center, width, density, color, light,
    cells, west, east, par, mix, center_here, width_here, density_here, color_here, light_here, sems,
):
    del first_slab, last_slab
    depth, rows, cols = vol.shape
    tiles = cols // LANES
    copies = [
        pltpu.make_async_copy(
            vol.at[:, :, pl.ds(t * LANES, LANES)], cells.at[t, :, pl.ds(SUB, rows)], sems.at[t]
        )
        for t in range(tiles)
    ]
    small = [
        pltpu.make_async_copy(src, dst, sems.at[tiles + i])
        for i, (src, dst) in enumerate((
            (center, center_here), (width, width_here), (density, density_here),
            (color, color_here), (light, light_here),
        ))
    ]
    for copy in small + copies:
        copy.start()
    log2e = math.log2(math.e)

    def spread(ref, row, k, lanes=LANES):
        return jnp.broadcast_to(ref[pl.ds(row, 1), pl.ds(k, 1)], (SUB, lanes))

    border = jnp.zeros((tiles, depth, SUB, LANES), jnp.float32)
    cells[:, :, pl.ds(0, SUB), :] = border
    cells[:, :, pl.ds(SUB + rows, SUB), :] = border
    for copy in small:
        copy.wait()
    wide = lax.broadcasted_iota(jnp.int32, (SUB, MIX), 1)
    row = lax.broadcasted_iota(jnp.int32, (SUB, MIX), 0)
    piece, pair, column = wide // 16, (wide // SUB) % 2, wide % SUB
    groups_of = [[], []]
    for k in range(BUMPS):
        scale = spread(width_here, 0, k, MIX)
        middle = spread(center_here, 0, k, MIX)
        dense = spread(density_here, 0, k, MIX) * (log2e / depth_all)
        a = -log2e / (scale * scale)
        parts_a = thirds(a)
        parts_b = thirds(-2.0 * a * middle)
        parts_c = thirds(a * middle * middle + jnp.log(dense) * log2e)
        value = jnp.zeros((SUB, MIX), jnp.float32)
        for first, parts in ((0, parts_a), (6, parts_b)):
            for at, which in enumerate((0, 1, 2, 0, 1, 0)):
                value = jnp.where(piece == first + at, parts[which], value)
        value = jnp.where(column == row, value, 0.0)
        for turn in range(3):
            hit = (piece == 12) & (column == (row + turn) % SUB)
            value = jnp.where(hit, parts_c[turn], value)
        for half in range(2):
            groups_of[half].append(jnp.where(pair == half, value, 0.0))
        dense = dense[:, :LANES]
        for c in range(3):
            par[SUB + c * BUMPS + k] = spread(color_here, c, k) / dense
    for half in range(2):
        for k in range(0, BUMPS, 2):
            both = jnp.concatenate(groups_of[half][k:k + 2], axis=0)
            mix[pl.ds((half * BUMPS + k) * SUB, 2 * SUB), :] = both.astype(jnp.bfloat16)
    for a in range(3):
        par[a] = spread(light_here, 0, a) * 0.7
    lane = lax.broadcasted_iota(jnp.int32, (SUB, LANES), 1)
    groups = west.shape[0]
    per_group = (rows // SUB) // groups

    def extract(t, source, out):
        def group(g, unused):
            packed = jnp.zeros((SUB, LANES), jnp.float32)
            for r in range(per_group):
                base = pl.multiple_of((g * per_group + r + 1) * SUB, SUB)
                for z in range(depth):
                    place = r * depth + z
                    tile = cells[t, z, pl.ds(base, SUB), :]
                    shift = (place - source) % LANES
                    moved = pltpu.roll(tile, shift, 1) if shift else tile
                    packed = jnp.where(lane == place, moved, packed)
            out[g] = packed
            return 0

        lax.fori_loop(0, groups, group, 0)

    copies[0].wait()
    extract(0, 0, west)
    for copy in copies[1:]:
        copy.wait()
    extract(tiles - 1, LANES - 1, east)


def prepare(depth_all, vol, *small):
    depth, rows, cols = vol.shape
    groups = -(-(rows // SUB) * depth // LANES)
    edge = jax.ShapeDtypeStruct((groups, SUB, LANES), jnp.float32)
    return pl.pallas_call(
        functools.partial(prepare_kernel, depth_all),
        out_shape=(
            jax.ShapeDtypeStruct((cols // LANES, depth, rows + 2 * SUB, LANES), jnp.float32),
            edge,
            edge,
            jax.ShapeDtypeStruct((SUB + 3 * BUMPS, SUB, LANES), jnp.float32),
            jax.ShapeDtypeStruct((2 * BUMPS * SUB, MIX), jnp.bfloat16),
        ),
        in_specs=[pl.BlockSpec(memory_space=pl.ANY)] * 8,
        out_specs=(VMEM,) * 5,
        scratch_shapes=[pltpu.VMEM(x.shape, jnp.float32) for x in small[-5:]]
        + [pltpu.SemaphoreType.DMA((cols // LANES + 5,))],
        compiler_params=pltpu.CompilerParams(vmem_limit_bytes=LIMIT),
        name="prepare",
    )(vol, *small)


def split(x):
    one = x.astype(jnp.bfloat16)
    rest = x - one.astype(jnp.float32)
    two = rest.astype(jnp.bfloat16)
    return one, two, (rest - two.astype(jnp.float32)).astype(jnp.bfloat16)


def march_kernel(away, extra, near, ys, zs, par, mix, cells, low, high, left, right, *refs):
    tiles, depth = cells.shape[:2]
    slab, column = lax.axis_index("depth"), lax.axis_index("col")
    here_z = lax.rem(slab, zs)
    has_low, has_high = slab > 0, slab < lax.axis_size("depth") - 1
    has_left, has_right = column > 0, column < lax.axis_size("col") - 1
    lane = lax.broadcasted_iota(jnp.int32, (SUB, LANES), 1)
    first = lane == 0
    last = lane == LANES - 1
    per_group = LANES // depth
    odd = lax.rem(here_z, 2)
    side = 2 * odd - 1
    origin, sign = (here_z - side, -side) if away else (here_z, side)
    targets = [lax.rem(origin + sign * d + zs, zs) for d in near]
    other, outs = (None, refs[extra:]) if away else (refs[0], refs[1 + extra:])
    ones = jnp.ones((2 * SUB, tiles * LANES), jnp.bfloat16)
    zeros = jnp.zeros((2 * SUB, tiles * LANES), jnp.bfloat16)

    def exponents(rb, p):
        base = pl.multiple_of(rb * SUB + SUB, SUB)
        pair = jnp.concatenate([
            jnp.concatenate(
                [cells[t, 2 * p + h, pl.ds(base, SUB), :] for t in range(tiles)], axis=1
            )
            for h in range(2)
        ], axis=0)
        v1, v2, v3 = split(pair)
        q1, q2, q3 = split(pair * pair)
        return jnp.dot(
            mix[...],
            jnp.concatenate(
                [q1, q1, q1, q2, q2, q3, v1, v1, v1, v2, v2, v3, ones, zeros, zeros, zeros], axis=0
            ),
            preferred_element_type=jnp.float32,
        )

    def block(rb):
        row = pl.multiple_of(rb * SUB, SUB)
        base = pl.multiple_of(rb * SUB + SUB, SUB)

        def cell(t, z, move=0):
            if z < 0 or z >= depth:
                beyond, inside = (low, has_low) if z < 0 else (high, has_high)
                return jnp.where(inside, beyond[pl.ds(row, SUB), pl.ds(t * LANES, LANES)], 0.0)
            return cells[t, z, pl.ds(base + move, SUB), :]

        group = lax.div(rb, per_group)
        turn = lax.rem(LANES - lax.rem(rb, per_group) * depth, LANES)
        halo_left = pltpu.roll(jnp.where(has_left, left[group], 0.0), turn, 1)
        halo_right = pltpu.roll(jnp.where(has_right, right[group], 0.0), turn, 1)
        acc = [[None] * BUMPS for t in range(tiles)]
        logt = [None] * tiles
        trans = [None] * tiles
        for z in range(depth):
            if z % 2 == 0:
                power = exponents(rb, z // 2)
            here = [cell(t, z) for t in range(tiles)]
            fwd = [pltpu.roll(h, 1, 1) for h in here]
            bwd = [pltpu.roll(h, LANES - 1, 1) for h in here]
            lo = halo_left if z == 0 else pltpu.roll(halo_left, LANES - z, 1)
            hi = pltpu.roll(halo_right, LANES - 1 - z, 1)
            for t in range(tiles):
                from_left = jnp.where(first, lo if t == 0 else fwd[t - 1], fwd[t])
                from_right = jnp.where(last, hi if t == tiles - 1 else bwd[t + 1], bwd[t])
                dx = from_right - from_left
                dy = cell(t, z, 1) - cell(t, z, -1)
                dz = cell(t, z + 1) - cell(t, z - 1)
                lit = jnp.abs(par[0] * dx + par[1] * dy + par[2] * dz)
                norm = (dx * dx + dy * dy) + (dz * dz + 4.0)
                shade = 0.3 + lit * lax.rsqrt(norm)
                lanes = slice(t * LANES, (t + 1) * LANES)
                top = (z % 2) * BUMPS * SUB
                b = [
                    jnp.exp2(power[top + k * SUB:top + (k + 1) * SUB, lanes])
                    for k in range(BUMPS)
                ]
                ext = ((b[0] + b[1]) + (b[2] + b[3])) + ((b[4] + b[5]) + (b[6] + b[7]))
                logt[t] = -ext if z == 0 else logt[t] - ext
                after = jnp.exp2(logt[t])
                weight = ((1.0 if z == 0 else trans[t]) - after) * shade
                trans[t] = after
                for k in range(BUMPS):
                    term = weight * b[k]
                    acc[t][k] = term if z == 0 else acc[t][k] + term
        totals = [[] for t in range(tiles)]
        for t in range(tiles):
            for c in range(3):
                total = acc[t][0] * par[SUB + c * BUMPS]
                for k in range(1, BUMPS):
                    total = total + acc[t][k] * par[SUB + c * BUMPS + k]
                totals[t].append(total)
            totals[t].append(logt[t])
        return totals

    unroll = max(1, min(ys, BODY // len(near)))

    def step(i, unused):
        for u in range(unroll):
            j = i * unroll + u
            for q in range(len(near)):
                for t, totals in enumerate(block(j * zs + targets[q])):
                    lanes = pl.ds(t * LANES, LANES)
                    if away:
                        for c in range(4):
                            outs[0][q, j, c, :, lanes] = totals[c]
                    else:
                        mate = [other[q, j, c, :, lanes] for c in range(4)]
                        ahead = [jnp.where(odd == 1, m, a) for a, m in zip(totals, mate)]
                        behind = [jnp.where(odd == 1, a, m) for a, m in zip(totals, mate)]
                        seen = jnp.exp2(ahead[3])
                        for c in range(3):
                            outs[q][j, c, :, lanes] = ahead[c] + seen * behind[c]
                        outs[q][j, 3, :, lanes] = ahead[3] + behind[3]
        return 0

    lax.fori_loop(0, ys // unroll, step, 0)


def march(name, near, ys, zs, par, mix, cells, low, high, left, right, other=None, after=()):
    tiles, depth = cells.shape[:2]
    away = other is None
    work = len(near) * ys * SUB * tiles * LANES * depth
    one = (ys, 4, SUB, tiles * LANES)
    if away:
        shapes = [jax.ShapeDtypeStruct((len(near),) + one, jnp.float32)]
    else:
        shapes = [jax.ShapeDtypeStruct(one, jnp.float32)] * len(near)
    operands = (par, mix, cells, low, high, left, right) + (() if away else (other,))
    return pl.pallas_call(
        functools.partial(march_kernel, away, len(after), near, ys, zs),
        out_shape=shapes,
        in_specs=[VMEM] * len(operands) + [pl.BlockSpec(memory_space=pl.ANY)] * len(after),
        out_specs=[VMEM] * len(shapes),
        compiler_params=pltpu.CompilerParams(vmem_limit_bytes=LIMIT),
        cost_estimate=pl.CostEstimate(
            flops=80 * work, bytes_accessed=4 * work, transcendentals=10 * work
        ),
        name=name,
    )(*operands, *after)


def over(parts, here):
    color, logt = [jnp.zeros_like(parts[0][0])] * 3, jnp.zeros_like(parts[0][3])
    back, back_logt = color, logt
    for s in reversed(range(len(parts))):
        turn = here == s
        back = [jnp.where(turn, a, b) for a, b in zip(color, back)]
        back_logt = jnp.where(turn, logt, back_logt)
        color = [jnp.where(turn, 0.0, a) for a in color]
        logt = jnp.where(turn, 0.0, logt)
        seen = jnp.exp2(logt)
        color = [a + seen * parts[s][c] for c, a in enumerate(color)]
        logt = logt + parts[s][3]
    seen = jnp.exp2(logt)
    return [a + seen * b for a, b in zip(color, back)], logt + back_logt


def hold(parts, work):
    anywhere = [pl.BlockSpec(memory_space=pl.ANY)] * len(parts)
    return pl.pallas_call(
        lambda *refs: None,
        out_shape=[jax.ShapeDtypeStruct(p.shape, p.dtype) for p in parts],
        in_specs=anywhere,
        out_specs=anywhere,
        input_output_aliases={i: i for i in range(len(parts))},
        compiler_params=pltpu.CompilerParams(vmem_limit_bytes=LIMIT),
        cost_estimate=pl.CostEstimate(flops=80 * work, bytes_accessed=4 * work, transcendentals=10 * work),
        name="hold",
    )(*parts)


def merge_z_kernel(ys, zs, *refs):
    pairs = len(refs) - ys
    parts, outs = refs[:pairs], refs[pairs:]
    me = lax.axis_index("depth")
    y, z = lax.div(me, zs), lax.rem(me, zs)
    odd = lax.rem(z, 2) == 1
    for t in range(ys):
        j = lax.rem(y + t, ys)
        held = [[p[j, c] for c in range(4)] for p in parts]
        ring = [held[0]] + [None] * (pairs - 1)
        for r in range(1, pairs):
            even_from = 2 * r - 1 if 2 * r <= pairs else 2 * (pairs - r)
            odd_from = 2 * r if 2 * r < pairs else 2 * (pairs - r) - 1
            ring[r] = [
                jnp.where(odd, a, b) for a, b in zip(held[odd_from], held[even_from])
            ]
        color, logt = over(ring, lax.div(z, 2))
        for c in range(3):
            outs[t][c] = color[c]
        outs[t][3] = logt


def merge_z(ys, zs, parts):
    shape = parts[0].shape[1:]
    return pl.pallas_call(
        functools.partial(merge_z_kernel, ys, zs),
        out_shape=[jax.ShapeDtypeStruct(shape, jnp.float32)] * ys,
        in_specs=[VMEM] * len(parts),
        out_specs=[VMEM] * ys,
        compiler_params=pltpu.CompilerParams(vmem_limit_bytes=LIMIT),
        name="merge_z",
    )(*parts)


def merge_y_kernel(zs, *refs):
    parts, out = refs[:-1], refs[-1]
    y = lax.div(lax.axis_index("depth"), zs)
    color, logt = over([[p[c] for c in range(4)] for p in parts], y)
    for c in range(3):
        out[c] = color[c]
    out[3] = 1.0 - jnp.exp2(logt)


def merge_y(zs, parts):
    return pl.pallas_call(
        functools.partial(merge_y_kernel, zs),
        out_shape=jax.ShapeDtypeStruct(parts[0].shape, jnp.float32),
        in_specs=[VMEM] * len(parts),
        out_specs=VMEM,
        compiler_params=pltpu.CompilerParams(vmem_limit_bytes=LIMIT),
        name="merge_y",
    )(*parts)


def in_hbm(x):
    return pltpu.with_memory_space_constraint(x, pltpu.HBM)


def on_device(volume, tf_center, tf_width, tf_density, tf_color, light):
    depth, rows, cols = volume.shape
    slabs = lax.axis_size("depth")
    ys, zs = split_depth(slabs)
    depth_all = depth * slabs
    up = [(i, (i + 1) % slabs) for i in range(slabs)]
    down = [(j, i) for i, j in up]
    first_slab, last_slab = volume[0], volume[depth - 1]
    low = lax.ppermute(last_slab, "depth", up)
    high = lax.ppermute(first_slab, "depth", down)
    cells, west_edge, east_edge, par, mix = prepare(
        depth_all, in_hbm(volume), first_slab, last_slab, in_hbm(tf_center[None]),
        in_hbm(tf_width[None]), in_hbm(tf_density[None]), in_hbm(tf_color), in_hbm(light[None]),
    )
    width = lax.axis_size("col")
    east = [(i, (i + 1) % width) for i in range(width)]
    west = [(j, i) for i, j in east]
    left = lax.ppermute(east_edge, "col", east)
    right = lax.ppermute(west_edge, "col", west)

    def along_z(x, to):
        return lax.ppermute(
            x, "depth", [(y * zs + z, y * zs + to(z) % zs) for y in range(ys) for z in range(zs)]
        )

    common = (ys, zs, par, mix, cells, low, high, left, right)
    reach = (zs - 2) // 2
    far = list(range(reach, 0, -1)) + [0]
    stages = [far[:2], far[2:]] if len(far) > 2 else [far]
    given, after = [], ()
    for i, near in enumerate(stages):
        parts = march("away%d" % i, near, *common, after=after)[0]
        given.append(along_z(parts, lambda z: z ^ 1))
        after = (parts,)
    arrived = [None] * (reach + 1)
    for i, near in enumerate(stages):
        parts = march("keep%d" % i, near, *common, other=given[i], after=after)
        for d, part in zip(near, parts):
            arrived[d] = along_z(part, lambda z: z + d if z % 2 else z - d) if d else part
        after = (parts[0],)
    early = [d for d in stages[0] if d] if len(stages) > 1 else []
    for d, part in zip(early, hold([arrived[d] for d in early], 16 * arrived[0].size) if early else []):
        arrived[d] = part
    merged = list(merge_z(ys, zs, arrived))
    for t in range(1, ys):
        pairs = [(i, (i + t * zs) % slabs) for i in range(slabs)]
        merged[t] = lax.ppermute(merged[t], "depth", pairs)
    return merge_y(zs, merged)


def solution(mesh):
    return jax.shard_map(
        on_device,
        mesh=mesh,
        in_specs=(P("depth", None, "col"), P(), P(), P(), P(), P()),
        out_specs=P(None, "depth", "col"),
        check_vma=False,
    )
```

time: 67.3 us -> 56.4 us (0.84)
  starting transfers between devices: 38.4 us -> 22.5 us
  waiting for transfers between devices: 7.25 us -> 15.3 us
  Pallas kernels: 20 us -> 17.3 us
    ppermute x7 -> x5, starting transfers between devices: 21.8 us -> 7.5 us  [along_z(): lax.ppermute(x, 'depth', [(y * zs + z, y * zs + to(z) % zs) for y in rang...]
    ppermute x7 -> x5, waiting for transfers between devices: 3.27 us -> 9.67 us  [along_z(): lax.ppermute(x, 'depth', [(y * zs + z, y * zs + to(z) % zs) for y in rang...]
    ppermute x1, starting transfers between devices: 1.29 us -> 6.48 us  [on_device(): high = lax.ppermute(first_slab, 'depth', down)]
    pallas_call x4 -> x5, Pallas kernels: 15.8 us -> 13.2 us  [the longest x4 13.2 us: march(): pl.pallas_call(functools.partial(march_kernel, away, len(after), near, ys...]
    ppermute x1, starting transfers between devices: 3.64 us -> 1.73 us  [on_device(): right = lax.ppermute(west_edge, 'col', west)]
    ppermute x1, starting transfers between devices: 1.92 us -> 0.02 us  [on_device(): left = lax.ppermute(east_edge, 'col', east)]
    ppermute x1, starting transfers between devices: 3.84 us -> 1.99 us  [on_device(): low = lax.ppermute(last_slab, 'depth', up)]
    ppermute x3, waiting for transfers between devices: 2.56 us -> 4.17 us  [on_device(): merged[t] = lax.ppermute(merged[t], 'depth', pairs)]
  transfers between devices with their start and end apart: 14 -> 12, of which waited for: 4 -> 8; matrix products, arithmetic and copies ran while one was open for 0% -> 0% of each run, Pallas kernels for 26% -> 24%
where the time goes in v3:
time: 56.4 us; the launch traced here: 56.3 us
  starting transfers between devices  22.5 us (40%)
  Pallas kernels  17.3 us (31%)
  waiting for transfers between devices  15.3 us (27%)
  local copies, waits for them, and re-layouts  1.06 us (2%)
    pallas_call x4, Pallas kernels, march(): pl.pallas_call(functools.partial(march_kernel, away, len(after), near, ys...  13.2 us
    ppermute x5, waiting for transfers between devices, along_z(): lax.ppermute(x, 'depth', [(y * zs + z, y * zs + to(z) % zs) for y in rang...  9.67 us
    ppermute x5, starting transfers between devices, along_z(): lax.ppermute(x, 'depth', [(y * zs + z, y * zs + to(z) % zs) for y in rang...  7.5 us
    ppermute x1, starting transfers between devices, on_device(): high = lax.ppermute(first_slab, 'depth', down)  6.48 us
    ppermute x3, starting transfers between devices, on_device(): merged[t] = lax.ppermute(merged[t], 'depth', pairs)  4.8 us
    ppermute x3, waiting for transfers between devices, on_device(): merged[t] = lax.ppermute(merged[t], 'depth', pairs)  4.17 us
    pallas_call x1, Pallas kernels, prepare(): pl.pallas_call(functools.partial(prepare_kernel, depth_all), out_shape=(j...  3.39 us
    ppermute x1, starting transfers between devices, on_device(): low = lax.ppermute(last_slab, 'depth', up)  1.99 us
  transfers between devices with their start and end apart: 12, of which 8 were waited for; matrix products, arithmetic and copies ran while one was open for 0% of the time, Pallas kernels for 24%

profile of v3, /device:TPU:4, one launch (start us, length us, event | category | flops | bytes accessed | tf_op | source)
XLA Modules:
  0.0 56.3 jit_solution(1429664079439836688)
XLA Ops:
  0.0 1.1 %slice_bitcast_fusion = (f32[256,256]{1,0:T(8,128)S(1)}, f32[256,256]{1,0:T(8,128)S(1)}) fusion(f32[16,256,256]{2,1,0:T(8,128)} %vol.1), kind=kLoop, calls=%fused_computation | loop fusion | bytes 1048576 | tf_op jit(solution)/shard_map/squeeze | solution.py:387
  1.1 2.0 %collective-permute-start = (f32[256,256]{1,0:T(8,128)S(1)}, f32[256,256]{1,0:T(8,128)S(1)}, u32[]{:S(2)}, u32[]{:S(2)}) collective-permute-start(f32[256,256]{1,0:T(8,128)S(1)} %get-tuple-element.35.last_slab), channel_id=1, source_target_pairs={{0,8},{8,16},{16,24},{24,32},{32,40},{40,48},{48,56},{56,64},{64,7... | collective-permute-start | bytes 786440 | tf_op jit(solution)/shard_map/ppermute | solution.py:388
  3.1 6.5 %collective-permute-start.1 = (f32[256,256]{1,0:T(8,128)S(1)}, f32[256,256]{1,0:T(8,128)S(1)}, u32[]{:S(2)}, u32[]{:S(2)}) collective-permute-start(f32[256,256]{1,0:T(8,128)S(1)} %get-tuple-element.36.first_slab), channel_id=1, source_target_pairs={{8,0},{16,8},{24,16},{32,24},{40,32},{48,40},{56,48},{64,56},{72,6... | collective-permute-start | bytes 786440 | tf_op jit(solution)/shard_map/ppermute | solution.py:389
  9.5 3.4 %prepare.1 = (f32[2,16,272,128]{3,2,1,0:T(8,128)S(1)}, f32[4,8,128]{2,1,0:T(8,128)S(1)}, f32[4,8,128]{2,1,0:T(8,128)S(1)}, f32[32,8,128]{2,1,0:T(8,128)S(1)}, bf16[128,256]{1,0:T(8,128)(2,1)S(1)}) custom-call(f32[16,256,256]{2,1,0:T(8,128)} %vol.1, f32[256,256]{1,0:T(8,128)S(1)} %get-tuple-element.36.first_slab, f32[256,256]{1,0:T(8,128)S(1)} %get-tuple-element.35.last_slab, ...), custom_call_target="tpu_custom_call" | custom-call | tf_op jit(solution)/shard_map/prepare/pallas_call | solution.py:126
  12.9 0.0 collective-permute-start.2
  13.0 1.7 %collective-permute-start.3 = (f32[4,8,128]{2,1,0:T(8,128)S(1)}, f32[4,8,128]{2,1,0:T(8,128)S(1)}, u32[]{:S(2)}, u32[]{:S(2)}) collective-permute-start(f32[4,8,128]{2,1,0:T(8,128)S(1)} %get-tuple-element.24), channel_id=1, source_target_pairs={{1,0},{2,1},{3,2},{4,3},{5,4},{6,5},{7,6},{0,7},{9,8},{10,9},{11,1... | collective-permute-start | bytes 49160 | tf_op jit(solution)/shard_map/ppermute | solution.py:398
  14.7 1.4 %collective-permute-done.2.left = f32[4,8,128]{2,1,0:T(8,128)S(1)} collective-permute-done((f32[4,8,128]{2,1,0:T(8,128)S(1)}, f32[4,8,128]{2,1,0:T(8,128)S(1)}, u32[]{:S(2)}, u32[]{:S(2)}) %collective-permute-start.2) | collective-permute-done | bytes 16416 | tf_op jit(solution)/shard_map/ppermute | solution.py:397
  16.1 0.0 collective-permute-done.3.right
  16.1 0.0 collective-permute-done.low
  16.1 0.0 collective-permute-done.1.high
  16.1 3.3 %away0.1.refs_0_ = f32[2,4,4,8,256]{4,3,2,1,0:T(8,128)S(1)} custom-call(f32[32,8,128]{2,1,0:T(8,128)S(1)} %get-tuple-element.20.par, bf16[128,256]{1,0:T(8,128)(2,1)S(1)} %get-tuple-element.21.mix, f32[2,16,272,128]{3,2,1,0:T(8,128)S(1)} %get-tuple-element.22.cells, f32[256,256]{1,0:T(8,128)S(1)} %collective-permute-done.low, ...), custom_call_target="tpu_custom_call" | custom-call | flops 20971520 | bytes 1048576 | tf_op jit(solution)/shard_map/away0/pallas_call | solution.py:279
  19.4 0.1 collective-permute-start.5
  19.5 3.3 %away1.1.refs_1_ = f32[2,4,4,8,256]{4,3,2,1,0:T(8,128)S(1)} custom-call(f32[32,8,128]{2,1,0:T(8,128)S(1)} %get-tuple-element.20.par, bf16[128,256]{1,0:T(8,128)(2,1)S(1)} %get-tuple-element.21.mix, f32[2,16,272,128]{3,2,1,0:T(8,128)S(1)} %get-tuple-element.22.cells, f32[256,256]{1,0:T(8,128)S(1)} %collective-permute-done.low, ...), custom_call_target="tpu_custom_call" | custom-call | flops 20971520 | bytes 1048576 | tf_op jit(solution)/shard_map/away1/pallas_call | solution.py:279
  22.9 1.9 %collective-permute-start.4 = (f32[2,4,4,8,256]{4,3,2,1,0:T(8,128)S(1)}, f32[2,4,4,8,256]{4,3,2,1,0:T(8,128)S(1)}, u32[]{:S(2)}, u32[]{:S(2)}) collective-permute-start(f32[2,4,4,8,256]{4,3,2,1,0:T(8,128)S(1)} %away1.1.refs_1_), channel_id=1, source_target_pairs={{0,8},{8,0},{16,24},{24,16},{32,40},{40,32},{48,56},{56,48},{64,72... | collective-permute-start | bytes 786440 | tf_op jit(solution)/shard_map/ppermute | solution.py:401
  24.8 3.6 %collective-permute-done.5.refs_0_ = f32[2,4,4,8,256]{4,3,2,1,0:T(8,128)S(1)} collective-permute-done((f32[2,4,4,8,256]{4,3,2,1,0:T(8,128)S(1)}, f32[2,4,4,8,256]{4,3,2,1,0:T(8,128)S(1)}, u32[]{:S(2)}, u32[]{:S(2)}) %collective-permute-start.5) | collective-permute-done | bytes 262176 | tf_op jit(solution)/shard_map/ppermute | solution.py:401
  28.4 3.4 %keep0.1 = (f32[4,4,8,256]{3,2,1,0:T(8,128)S(1)}, f32[4,4,8,256]{3,2,1,0:T(8,128)S(1)}) custom-call(f32[32,8,128]{2,1,0:T(8,128)S(1)} %get-tuple-element.20.par, bf16[128,256]{1,0:T(8,128)(2,1)S(1)} %get-tuple-element.21.mix, f32[2,16,272,128]{3,2,1,0:T(8,128)S(1)} %get-tuple-element.22.cells, f32[256,256]{1,0:T(8,128)S(1)} %collective-permute-done.low, ...), custom_call_target="tpu_custom_call" | custom-call | flops 20971520 | bytes 1048576 | tf_op jit(solution)/shard_map/keep0/pallas_call | solution.py:279
  31.7 0.5 collective-permute-start.7
  32.2 4.3 %collective-permute-start.8 = (f32[4,4,8,256]{3,2,1,0:T(8,128)S(1)}, f32[4,4,8,256]{3,2,1,0:T(8,128)S(1)}, u32[]{:S(2)}, u32[]{:S(2)}) collective-permute-start(f32[4,4,8,256]{3,2,1,0:T(8,128)S(1)} %get-tuple-element.28), channel_id=1, source_target_pairs={{0,48},{8,24},{16,0},{24,40},{32,16},{40,56},{48,32},{56,8},{64,11... | collective-permute-start | bytes 393224 | tf_op jit(solution)/shard_map/ppermute | solution.py:401
  36.5 0.0 collective-permute-done.4.refs_0_
  36.5 3.3 %keep1.1 = (f32[4,4,8,256]{3,2,1,0:T(8,128)S(1)}, f32[4,4,8,256]{3,2,1,0:T(8,128)S(1)}) custom-call(f32[32,8,128]{2,1,0:T(8,128)S(1)} %get-tuple-element.20.par, bf16[128,256]{1,0:T(8,128)(2,1)S(1)} %get-tuple-element.21.mix, f32[2,16,272,128]{3,2,1,0:T(8,128)S(1)} %get-tuple-element.22.cells, f32[256,256]{1,0:T(8,128)S(1)} %collective-permute-done.low, ...), custom_call_target="tpu_custom_call" | custom-call | flops 20971520 | bytes 1048576 | tf_op jit(solution)/shard_map/keep1/pallas_call | solution.py:279
  39.8 0.7 %collective-permute-start.6 = (f32[4,4,8,256]{3,2,1,0:T(8,128)S(1)}, f32[4,4,8,256]{3,2,1,0:T(8,128)S(1)}, u32[]{:S(2)}, u32[]{:S(2)}) collective-permute-start(f32[4,4,8,256]{3,2,1,0:T(8,128)S(1)} %get-tuple-element.27), channel_id=1, source_target_pairs={{0,56},{8,16},{16,8},{24,32},{32,24},{40,48},{48,40},{56,0},{64,12... | collective-permute-start | bytes 393224 | tf_op jit(solution)/shard_map/ppermute | solution.py:401
  40.5 2.5 %collective-permute-done.7.refs_0_ = f32[4,4,8,256]{3,2,1,0:T(8,128)S(1)} collective-permute-done((f32[4,4,8,256]{3,2,1,0:T(8,128)S(1)}, f32[4,4,8,256]{3,2,1,0:T(8,128)S(1)}, u32[]{:S(2)}, u32[]{:S(2)}) %collective-permute-start.7) | collective-permute-done | bytes 131104 | tf_op jit(solution)/shard_map/ppermute | solution.py:401
  43.0 1.8 %collective-permute-done.8.refs_1_ = f32[4,4,8,256]{3,2,1,0:T(8,128)S(1)} collective-permute-done((f32[4,4,8,256]{3,2,1,0:T(8,128)S(1)}, f32[4,4,8,256]{3,2,1,0:T(8,128)S(1)}, u32[]{:S(2)}, u32[]{:S(2)}) %collective-permute-start.8) | collective-permute-done | bytes 131104 | tf_op jit(solution)/shard_map/ppermute | solution.py:401
  44.8 1.8 %collective-permute-done.6.refs_1_ = f32[4,4,8,256]{3,2,1,0:T(8,128)S(1)} collective-permute-done((f32[4,4,8,256]{3,2,1,0:T(8,128)S(1)}, f32[4,4,8,256]{3,2,1,0:T(8,128)S(1)}, u32[]{:S(2)}, u32[]{:S(2)}) %collective-permute-start.6) | collective-permute-done | bytes 131104 | tf_op jit(solution)/shard_map/ppermute | solution.py:401
  46.6 0.1 merge_z.1
  46.7 2.8 %collective-permute-start.10 = (f32[4,8,256]{2,1,0:T(8,128)S(1)}, f32[4,8,256]{2,1,0:T(8,128)S(1)}, u32[]{:S(2)}, u32[]{:S(2)}) collective-permute-start(f32[4,8,256]{2,1,0:T(8,128)S(1)} %get-tuple-element.33), channel_id=1, source_target_pairs={{0,128},{8,136},{16,144},{24,152},{32,160},{40,168},{48,176},{56,1... | collective-permute-start | bytes 98312 | tf_op jit(solution)/shard_map/ppermute | solution.py:426
  49.4 1.1 %collective-permute-start.11 = (f32[4,8,256]{2,1,0:T(8,128)S(1)}, f32[4,8,256]{2,1,0:T(8,128)S(1)}, u32[]{:S(2)}, u32[]{:S(2)}) collective-permute-start(f32[4,8,256]{2,1,0:T(8,128)S(1)} %get-tuple-element.34), channel_id=1, source_target_pairs={{0,192},{8,200},{16,208},{24,216},{32,224},{40,232},{48,240},{56,2... | collective-permute-start | bytes 98312 | tf_op jit(solution)/shard_map/ppermute | solution.py:426
  50.5 1.0 %collective-permute-start.9 = (f32[4,8,256]{2,1,0:T(8,128)S(1)}, f32[4,8,256]{2,1,0:T(8,128)S(1)}, u32[]{:S(2)}, u32[]{:S(2)}) collective-permute-start(f32[4,8,256]{2,1,0:T(8,128)S(1)} %get-tuple-element.32), channel_id=1, source_target_pairs={{0,64},{8,72},{16,80},{24,88},{32,96},{40,104},{48,112},{56,120},{... | collective-permute-start | bytes 98312 | tf_op jit(solution)/shard_map/ppermute | solution.py:426
  51.5 0.7 %collective-permute-done.10.refs_2_ = f32[4,8,256]{2,1,0:T(8,128)S(1)} collective-permute-done((f32[4,8,256]{2,1,0:T(8,128)S(1)}, f32[4,8,256]{2,1,0:T(8,128)S(1)}, u32[]{:S(2)}, u32[]{:S(2)}) %collective-permute-start.10) | collective-permute-done | bytes 32800 | tf_op jit(solution)/shard_map/ppermute | solution.py:426
  52.2 1.2 %collective-permute-done.11.refs_3_ = f32[4,8,256]{2,1,0:T(8,128)S(1)} collective-permute-done((f32[4,8,256]{2,1,0:T(8,128)S(1)}, f32[4,8,256]{2,1,0:T(8,128)S(1)}, u32[]{:S(2)}, u32[]{:S(2)}) %collective-permute-start.11) | collective-permute-done | bytes 32800 | tf_op jit(solution)/shard_map/ppermute | solution.py:426
  53.3 2.3 %collective-permute-done.9.refs_1_ = f32[4,8,256]{2,1,0:T(8,128)S(1)} collective-permute-done((f32[4,8,256]{2,1,0:T(8,128)S(1)}, f32[4,8,256]{2,1,0:T(8,128)S(1)}, u32[]{:S(2)}, u32[]{:S(2)}) %collective-permute-start.9) | collective-permute-done | bytes 32800 | tf_op jit(solution)/shard_map/ppermute | solution.py:426
  55.6 0.6 %merge_y.1 = f32[4,8,256]{2,1,0:T(8,128)} custom-call(f32[4,8,256]{2,1,0:T(8,128)S(1)} %get-tuple-element.31.refs_0_, f32[4,8,256]{2,1,0:T(8,128)S(1)} %collective-permute-done.9.refs_1_, f32[4,8,256]{2,1,0:T(8,128)S(1)} %collective-permute-done.10.refs_2_, f32[4,8,256]{2,1,0:T(8,128)S(1)} %collective-permute-done.11.refs_3_), custom_call_target="tpu_custom_call" | custom-call | tf_op jit(solution)/shard_map/merge_y/pallas_call | solution.py:366
  (1 shorter events, 0.0 us)
Async XLA Ops:
  1.1 15.1 %collective-permute-start = (f32[256,256]{1,0:T(8,128)S(1)}, f32[256,256]{1,0:T(8,128)S(1)}, u32[]{:S(2)}, u32[]{:S(2)}) collective-permute-start(f32[256,256]{1,0:T(8,128)S(1)} %get-tuple-element.35.last_slab), channel_id=1, source_target_pairs={{0,8},{8,16},{16,24},{24,32},{32,40},{40,48},{48,56},{56,64},{64,7... | collective-permute-start | bytes 786440 | tf_op jit(solution)/shard_map/ppermute | solution.py:388
  3.1 13.1 %collective-permute-start.1 = (f32[256,256]{1,0:T(8,128)S(1)}, f32[256,256]{1,0:T(8,128)S(1)}, u32[]{:S(2)}, u32[]{:S(2)}) collective-permute-start(f32[256,256]{1,0:T(8,128)S(1)} %get-tuple-element.36.first_slab), channel_id=1, source_target_pairs={{8,0},{16,8},{24,16},{32,24},{40,32},{48,40},{56,48},{64,56},{72,6... | collective-permute-start | bytes 786440 | tf_op jit(solution)/shard_map/ppermute | solution.py:389
  12.9 3.2 %collective-permute-start.2 = (f32[4,8,128]{2,1,0:T(8,128)S(1)}, f32[4,8,128]{2,1,0:T(8,128)S(1)}, u32[]{:S(2)}, u32[]{:S(2)}) collective-permute-start(f32[4,8,128]{2,1,0:T(8,128)S(1)} %get-tuple-element.23), channel_id=1, source_target_pairs={{0,1},{1,2},{2,3},{3,4},{4,5},{5,6},{6,7},{7,0},{8,9},{9,10},{10,1... | collective-permute-start | bytes 49160 | tf_op jit(solution)/shard_map/ppermute | solution.py:397
  13.0 3.2 %collective-permute-start.3 = (f32[4,8,128]{2,1,0:T(8,128)S(1)}, f32[4,8,128]{2,1,0:T(8,128)S(1)}, u32[]{:S(2)}, u32[]{:S(2)}) collective-permute-start(f32[4,8,128]{2,1,0:T(8,128)S(1)} %get-tuple-element.24), channel_id=1, source_target_pairs={{1,0},{2,1},{3,2},{4,3},{5,4},{6,5},{7,6},{0,7},{9,8},{10,9},{11,1... | collective-permute-start | bytes 49160 | tf_op jit(solution)/shard_map/ppermute | solution.py:398
  19.4 8.9 %collective-permute-start.5 = (f32[2,4,4,8,256]{4,3,2,1,0:T(8,128)S(1)}, f32[2,4,4,8,256]{4,3,2,1,0:T(8,128)S(1)}, u32[]{:S(2)}, u32[]{:S(2)}) collective-permute-start(f32[2,4,4,8,256]{4,3,2,1,0:T(8,128)S(1)} %away0.1.refs_0_), channel_id=1, source_target_pairs={{0,8},{8,0},{16,24},{24,16},{32,40},{40,32},{48,56},{56,48},{64,72... | collective-permute-start | bytes 786440 | tf_op jit(solution)/shard_map/ppermute | solution.py:401
  22.9 13.7 %collective-permute-start.4 = (f32[2,4,4,8,256]{4,3,2,1,0:T(8,128)S(1)}, f32[2,4,4,8,256]{4,3,2,1,0:T(8,128)S(1)}, u32[]{:S(2)}, u32[]{:S(2)}) collective-permute-start(f32[2,4,4,8,256]{4,3,2,1,0:T(8,128)S(1)} %away1.1.refs_1_), channel_id=1, source_target_pairs={{0,8},{8,0},{16,24},{24,16},{32,40},{40,32},{48,56},{56,48},{64,72... | collective-permute-start | bytes 786440 | tf_op jit(solution)/shard_map/ppermute | solution.py:401
  31.7 11.2 %collective-permute-start.7 = (f32[4,4,8,256]{3,2,1,0:T(8,128)S(1)}, f32[4,4,8,256]{3,2,1,0:T(8,128)S(1)}, u32[]{:S(2)}, u32[]{:S(2)}) collective-permute-start(f32[4,4,8,256]{3,2,1,0:T(8,128)S(1)} %get-tuple-element.25.refs_1_), channel_id=1, source_target_pairs={{0,40},{8,32},{16,56},{24,48},{32,8},{40,0},{48,24},{56,16},{64,10... | collective-permute-start | bytes 393224 | tf_op jit(solution)/shard_map/ppermute | solution.py:401
  32.2 12.6 %collective-permute-start.8 = (f32[4,4,8,256]{3,2,1,0:T(8,128)S(1)}, f32[4,4,8,256]{3,2,1,0:T(8,128)S(1)}, u32[]{:S(2)}, u32[]{:S(2)}) collective-permute-start(f32[4,4,8,256]{3,2,1,0:T(8,128)S(1)} %get-tuple-element.28), channel_id=1, source_target_pairs={{0,48},{8,24},{16,0},{24,40},{32,16},{40,56},{48,32},{56,8},{64,11... | collective-permute-start | bytes 393224 | tf_op jit(solution)/shard_map/ppermute | solution.py:401
  39.8 6.8 %collective-permute-start.6 = (f32[4,4,8,256]{3,2,1,0:T(8,128)S(1)}, f32[4,4,8,256]{3,2,1,0:T(8,128)S(1)}, u32[]{:S(2)}, u32[]{:S(2)}) collective-permute-start(f32[4,4,8,256]{3,2,1,0:T(8,128)S(1)} %get-tuple-element.27), channel_id=1, source_target_pairs={{0,56},{8,16},{16,8},{24,32},{32,24},{40,48},{48,40},{56,0},{64,12... | collective-permute-start | bytes 393224 | tf_op jit(solution)/shard_map/ppermute | solution.py:401
  46.7 5.5 %collective-permute-start.10 = (f32[4,8,256]{2,1,0:T(8,128)S(1)}, f32[4,8,256]{2,1,0:T(8,128)S(1)}, u32[]{:S(2)}, u32[]{:S(2)}) collective-permute-start(f32[4,8,256]{2,1,0:T(8,128)S(1)} %get-tuple-element.33), channel_id=1, source_target_pairs={{0,128},{8,136},{16,144},{24,152},{32,160},{40,168},{48,176},{56,1... | collective-permute-start | bytes 98312 | tf_op jit(solution)/shard_map/ppermute | solution.py:426
  49.4 3.9 %collective-permute-start.11 = (f32[4,8,256]{2,1,0:T(8,128)S(1)}, f32[4,8,256]{2,1,0:T(8,128)S(1)}, u32[]{:S(2)}, u32[]{:S(2)}) collective-permute-start(f32[4,8,256]{2,1,0:T(8,128)S(1)} %get-tuple-element.34), channel_id=1, source_target_pairs={{0,192},{8,200},{16,208},{24,216},{32,224},{40,232},{48,240},{56,2... | collective-permute-start | bytes 98312 | tf_op jit(solution)/shard_map/ppermute | solution.py:426
  50.5 5.1 %collective-permute-start.9 = (f32[4,8,256]{2,1,0:T(8,128)S(1)}, f32[4,8,256]{2,1,0:T(8,128)S(1)}, u32[]{:S(2)}, u32[]{:S(2)}) collective-permute-start(f32[4,8,256]{2,1,0:T(8,128)S(1)} %get-tuple-element.32), channel_id=1, source_target_pairs={{0,64},{8,72},{16,80},{24,88},{32,96},{40,104},{48,112},{56,120},{... | collective-permute-start | bytes 98312 | tf_op jit(solution)/shard_map/ppermute | solution.py:426

commit v4 on v3

--- a/solution.py
+++ b/solution.py
@@ -36,14 +36,21 @@
     del first_slab, last_slab
     depth, rows, cols = vol.shape
     tiles = cols // LANES
-    copies = [
-        pltpu.make_async_copy(
-            vol.at[:, :, pl.ds(t * LANES, LANES)], cells.at[t, :, pl.ds(SUB, rows)], sems.at[t]
+    groups = west.shape[0]
+    band = rows // groups
+
+    def load(t, g):
+        return pltpu.make_async_copy(
+            vol.at[:, pl.ds(g * band, band), pl.ds(t * LANES, LANES)],
+            cells.at[t, :, pl.ds(SUB + g * band, band)],
+            sems.at[t * groups + g],
         )
-        for t in range(tiles)
-    ]
+
+    edges = list(dict.fromkeys((0, tiles - 1)))
+    order = edges + [t for t in range(tiles) if t not in edges]
+    copies = [load(t, g) for g in range(groups) for t in order]
     small = [
-        pltpu.make_async_copy(src, dst, sems.at[tiles + i])
+        pltpu.make_async_copy(src, dst, sems.at[tiles * groups + i])
         for i, (src, dst) in enumerate((
             (center, center_here), (width, width_here), (density, density_here),
             (color, color_here), (light, light_here),
@@ -93,30 +100,25 @@
     for a in range(3):
         par[a] = spread(light_here, 0, a) * 0.7
     lane = lax.broadcasted_iota(jnp.int32, (SUB, LANES), 1)
-    groups = west.shape[0]
-    per_group = (rows // SUB) // groups
-
-    def extract(t, source, out):
-        def group(g, unused):
-            packed = jnp.zeros((SUB, LANES), jnp.float32)
-            for r in range(per_group):
-                base = pl.multiple_of((g * per_group + r + 1) * SUB, SUB)
-                for z in range(depth):
-                    place = r * depth + z
-                    tile = cells[t, z, pl.ds(base, SUB), :]
-                    shift = (place - source) % LANES
-                    moved = pltpu.roll(tile, shift, 1) if shift else tile
-                    packed = jnp.where(lane == place, moved, packed)
-            out[g] = packed
-            return 0
-
-        lax.fori_loop(0, groups, group, 0)
-
-    copies[0].wait()
-    extract(0, 0, west)
-    for copy in copies[1:]:
-        copy.wait()
-    extract(tiles - 1, LANES - 1, east)
+    per_group = band // SUB
+
+    def extract(t, g, source, out):
+        packed = jnp.zeros((SUB, LANES), jnp.float32)
+        for r in range(per_group):
+            for z in range(depth):
+                place = r * depth + z
+                tile = cells[t, z, pl.ds((g * per_group + r + 1) * SUB, SUB), :]
+                shift = (place - source) % LANES
+                moved = pltpu.roll(tile, shift, 1) if shift else tile
+                packed = jnp.where(lane == place, moved, packed)
+        out[g] = packed
+
+    waits = iter(copies)
+    for g in range(groups):
+        for t in order:
+            next(waits).wait()
+        extract(0, g, 0, west)
+        extract(tiles - 1, g, LANES - 1, east)
 
 
 def prepare(depth_all, vol, *small):
@@ -135,7 +137,7 @@
         in_specs=[pl.BlockSpec(memory_space=pl.ANY)] * 8,
         out_specs=(VMEM,) * 5,
         scratch_shapes=[pltpu.VMEM(x.shape, jnp.float32) for x in small[-5:]]
-        + [pltpu.SemaphoreType.DMA((cols // LANES + 5,))],
+        + [pltpu.SemaphoreType.DMA((cols // LANES * groups + 5,))],
         compiler_params=pltpu.CompilerParams(vmem_limit_bytes=LIMIT),
         name="prepare",
     )(vol, *small)
@@ -148,7 +150,7 @@
     return one, two, (rest - two.astype(jnp.float32)).astype(jnp.bfloat16)
 
 
-def march_kernel(away, extra, near, ys, zs, par, mix, cells, low, high, left, right, *refs):
+def march_kernel(away, slot, extra, near, ys, zs, par, mix, cells, low, high, left, right, *refs):
     tiles, depth = cells.shape[:2]
     slab, column = lax.axis_index("depth"), lax.axis_index("col")
     here_z = lax.rem(slab, zs)
@@ -162,7 +164,7 @@
     side = 2 * odd - 1
     origin, sign = (here_z - side, -side) if away else (here_z, side)
     targets = [lax.rem(origin + sign * d + zs, zs) for d in near]
-    other, outs = (None, refs[extra:]) if away else (refs[0], refs[1 + extra:])
+    other, outs = (None, refs[extra:]) if slot is None else (refs[0], refs[1 + extra:])
     ones = jnp.ones((2 * SUB, tiles * LANES), jnp.bfloat16)
     zeros = jnp.zeros((2 * SUB, tiles * LANES), jnp.bfloat16)
 
@@ -250,43 +252,40 @@
             for q in range(len(near)):
                 for t, totals in enumerate(block(j * zs + targets[q])):
                     lanes = pl.ds(t * LANES, LANES)
-                    if away:
-                        for c in range(4):
-                            outs[0][q, j, c, :, lanes] = totals[c]
-                    else:
-                        mate = [other[q, j, c, :, lanes] for c in range(4)]
-                        ahead = [jnp.where(odd == 1, m, a) for a, m in zip(totals, mate)]
-                        behind = [jnp.where(odd == 1, a, m) for a, m in zip(totals, mate)]
-                        seen = jnp.exp2(ahead[3])
-                        for c in range(3):
-                            outs[q][j, c, :, lanes] = ahead[c] + seen * behind[c]
-                        outs[q][j, 3, :, lanes] = ahead[3] + behind[3]
+                    if other is not None:
+                        mate = [other[slot + q, j, c, :, lanes] for c in range(4)]
+                        totals = pair_over(totals, mate, odd == 1)
+                    for c in range(4):
+                        outs[0][q, j, c, :, lanes] = totals[c]
         return 0
 
     lax.fori_loop(0, ys // unroll, step, 0)
 
 
-def march(name, near, ys, zs, par, mix, cells, low, high, left, right, other=None, after=()):
+def march(name, away, near, ys, zs, par, mix, cells, low, high, left, right, other=None, after=()):
     tiles, depth = cells.shape[:2]
-    away = other is None
     work = len(near) * ys * SUB * tiles * LANES * depth
-    one = (ys, 4, SUB, tiles * LANES)
-    if away:
-        shapes = [jax.ShapeDtypeStruct((len(near),) + one, jnp.float32)]
-    else:
-        shapes = [jax.ShapeDtypeStruct(one, jnp.float32)] * len(near)
-    operands = (par, mix, cells, low, high, left, right) + (() if away else (other,))
+    shape = (len(near), ys, 4, SUB, tiles * LANES)
+    mate, slot = ((), None) if other is None else ((other[0],), other[1])
+    operands = (par, mix, cells, low, high, left, right) + mate
     return pl.pallas_call(
-        functools.partial(march_kernel, away, len(after), near, ys, zs),
-        out_shape=shapes,
+        functools.partial(march_kernel, away, slot, len(after), near, ys, zs),
+        out_shape=jax.ShapeDtypeStruct(shape, jnp.float32),
         in_specs=[VMEM] * len(operands) + [pl.BlockSpec(memory_space=pl.ANY)] * len(after),
-        out_specs=[VMEM] * len(shapes),
+        out_specs=VMEM,
         compiler_params=pltpu.CompilerParams(vmem_limit_bytes=LIMIT),
         cost_estimate=pl.CostEstimate(
             flops=80 * work, bytes_accessed=4 * work, transcendentals=10 * work
         ),
         name=name,
     )(*operands, *after)
+
+
+def pair_over(own, mate, mate_nearer):
+    ahead = [jnp.where(mate_nearer, m, a) for a, m in zip(own, mate)]
+    behind = [jnp.where(mate_nearer, a, m) for a, m in zip(own, mate)]
+    seen = jnp.exp2(ahead[3])
+    return [a + seen * b for a, b in zip(ahead[:3], behind[:3])] + [ahead[3] + behind[3]]
 
 
 def over(parts, here):
@@ -320,14 +319,20 @@
 
 
 def merge_z_kernel(ys, zs, *refs):
-    pairs = len(refs) - ys
-    parts, outs = refs[:pairs], refs[pairs:]
+    pairs = zs // 2
+    loose = 2 * min(2, pairs)
+    singles, parts, outs = refs[:loose], refs[loose:-ys], refs[-ys:]
     me = lax.axis_index("depth")
     y, z = lax.div(me, zs), lax.rem(me, zs)
     odd = lax.rem(z, 2) == 1
     for t in range(ys):
         j = lax.rem(y + t, ys)
-        held = [[p[j, c] for c in range(4)] for p in parts]
+        held = [[p[0, j, c] for c in range(4)] for p in singles]
+        held = [
+            pair_over(held[i], held[i + 1], odd if i == 0 else jnp.logical_not(odd))
+            for i in range(0, loose, 2)
+        ]
+        held += [[p[0, j, c] for c in range(4)] for p in parts]
         ring = [held[0]] + [None] * (pairs - 1)
         for r in range(1, pairs):
             even_from = 2 * r - 1 if 2 * r <= pairs else 2 * (pairs - r)
@@ -342,7 +347,7 @@
 
 
 def merge_z(ys, zs, parts):
-    shape = parts[0].shape[1:]
+    shape = parts[0].shape[2:]
     return pl.pallas_call(
         functools.partial(merge_z_kernel, ys, zs),
         out_shape=[jax.ShapeDtypeStruct(shape, jnp.float32)] * ys,
@@ -404,23 +409,31 @@
 
     common = (ys, zs, par, mix, cells, low, high, left, right)
     reach = (zs - 2) // 2
-    far = list(range(reach, 0, -1)) + [0]
-    stages = [far[:2], far[2:]] if len(far) > 2 else [far]
-    given, after = [], ()
-    for i, near in enumerate(stages):
-        parts = march("away%d" % i, near, *common, after=after)[0]
-        given.append(along_z(parts, lambda z: z ^ 1))
+    far = list(range(reach, 1, -1))
+    after, incoming = (), {}
+
+    def step(name, away, near, other=None):
+        nonlocal after
+        parts = march(name, away, near, *common, other=other, after=after)
         after = (parts,)
-    arrived = [None] * (reach + 1)
-    for i, near in enumerate(stages):
-        parts = march("keep%d" % i, near, *common, other=given[i], after=after)
-        for d, part in zip(near, parts):
-            arrived[d] = along_z(part, lambda z: z + d if z % 2 else z - d) if d else part
-        after = (parts[0],)
-    early = [d for d in stages[0] if d] if len(stages) > 1 else []
-    for d, part in zip(early, hold([arrived[d] for d in early], 16 * arrived[0].size) if early else []):
-        arrived[d] = part
-    merged = list(merge_z(ys, zs, arrived))
+        return parts
+
+    if far:
+        given = along_z(step("away", True, far), lambda z: z ^ 1)
+    if reach:
+        incoming["near"] = along_z(step("near", False, [1]), lambda z: z + 1 if z % 2 else z - 1)
+        incoming["past"] = along_z(step("past", True, [1]), lambda z: z - 2 if z % 2 else z + 2)
+    for slot, d in enumerate(far):
+        parts = step("keep%d" % d, False, [d], other=(given, slot))
+        incoming[d] = along_z(parts, lambda z: z + d if z % 2 else z - d)
+    mate = along_z(step("mate", True, [0]), lambda z: z ^ 1)
+    own = step("own", False, [0])
+    for count in range(1, len(incoming) + 1):
+        early = list(incoming)[:count]
+        for key, part in zip(early, hold([incoming[key] for key in early], 16 * own.size)):
+            incoming[key] = part
+    loose = [own, mate] + ([incoming["near"], incoming["past"]] if reach else [])
+    merged = list(merge_z(ys, zs, loose + [incoming[d] for d in reversed(far)]))
     for t in range(1, ys):
         pairs = [(i, (i + t * zs) % slabs) for i in range(slabs)]
         merged[t] = lax.ppermute(merged[t], "depth", pairs)

time: 56.4 us -> 51.8 us (0.918); the launches traced: 56.3 us -> 51 us
  waiting for transfers between devices: 15.3 us -> 10.2 us
  Pallas kernels: 17.3 us -> 16.7 us
    ppermute x5 -> x6, waiting for transfers between devices: 9.67 us -> 6.45 us  [along_z(): lax.ppermute(x, 'depth', [(y * zs + z, y * zs + to(z) % zs) for y in rang...]
    ppermute x3, waiting for transfers between devices: 4.17 us -> 2.05 us  [on_device(): merged[t] = lax.ppermute(merged[t], 'depth', pairs)]
    ppermute x3, starting transfers between devices: 4.8 us -> 5.67 us  [on_device(): merged[t] = lax.ppermute(merged[t], 'depth', pairs)]
    pallas_call x1, Pallas kernels: 3.39 us -> 2.77 us  [prepare(): pl.pallas_call(functools.partial(prepare_kernel, depth_all), out_shape=(j...]
    ppermute x5 -> x6, starting transfers between devices: 7.5 us -> 7.07 us  [along_z(): lax.ppermute(x, 'depth', [(y * zs + z, y * zs + to(z) % zs) for y in rang...]
    pallas_call x4 -> x7, Pallas kernels: 13.2 us -> 13.2 us  [march(): pl.pallas_call(functools.partial(march_kernel, away, slot, len(after), ne...]
  transfers between devices with their start and end apart: 12 -> 13, of which waited for: 8 -> 8; matrix products, arithmetic and copies ran while one was open for 0% -> 0% of each run, Pallas kernels for 24% -> 25%
where the time goes in v4:
time: 51.8 us; the launch traced here: 51 us
  starting transfers between devices  23 us (44%)
  Pallas kernels  16.7 us (32%)
  waiting for transfers between devices  10.2 us (20%)
  local copies, waits for them, and re-layouts  1.06 us (2%)
    pallas_call x7, Pallas kernels, march(): pl.pallas_call(functools.partial(march_kernel, away, slot, len(after), ne...  13.2 us
    ppermute x6, starting transfers between devices, along_z(): lax.ppermute(x, 'depth', [(y * zs + z, y * zs + to(z) % zs) for y in rang...  7.07 us
    ppermute x1, starting transfers between devices, on_device(): high = lax.ppermute(first_slab, 'depth', down)  6.48 us
    ppermute x6, waiting for transfers between devices, along_z(): lax.ppermute(x, 'depth', [(y * zs + z, y * zs + to(z) % zs) for y in rang...  6.45 us
    ppermute x3, starting transfers between devices, on_device(): merged[t] = lax.ppermute(merged[t], 'depth', pairs)  5.67 us
    pallas_call x1, Pallas kernels, prepare(): pl.pallas_call(functools.partial(prepare_kernel, depth_all), out_shape=(j...  2.77 us
    ppermute x3, waiting for transfers between devices, on_device(): merged[t] = lax.ppermute(merged[t], 'depth', pairs)  2.05 us
    ppermute x1, starting transfers between devices, on_device(): low = lax.ppermute(last_slab, 'depth', up)  1.99 us
  transfers between devices with their start and end apart: 13, of which 8 were waited for; matrix products, arithmetic and copies ran while one was open for 0% of the time, Pallas kernels for 25%

profile of v4, /device:TPU:4, one launch (start us, length us, event | category | flops | bytes accessed | tf_op | source)
XLA Modules:
  0.0 51.0 jit_solution(4625227502298967966)
XLA Ops:
  0.0 1.1 %slice_bitcast_fusion = (f32[256,256]{1,0:T(8,128)S(1)}, f32[256,256]{1,0:T(8,128)S(1)}) fusion(f32[16,256,256]{2,1,0:T(8,128)} %vol.1), kind=kLoop, calls=%fused_computation | loop fusion | bytes 1048576 | tf_op jit(solution)/shard_map/squeeze | solution.py:392
  1.1 2.0 %collective-permute-start = (f32[256,256]{1,0:T(8,128)S(1)}, f32[256,256]{1,0:T(8,128)S(1)}, u32[]{:S(2)}, u32[]{:S(2)}) collective-permute-start(f32[256,256]{1,0:T(8,128)S(1)} %get-tuple-element.41.last_slab), channel_id=1, source_target_pairs={{0,8},{8,16},{16,24},{24,32},{32,40},{40,48},{48,56},{56,64},{64,7... | collective-permute-start | bytes 786440 | tf_op jit(solution)/shard_map/ppermute | solution.py:393
  3.1 6.5 %collective-permute-start.1 = (f32[256,256]{1,0:T(8,128)S(1)}, f32[256,256]{1,0:T(8,128)S(1)}, u32[]{:S(2)}, u32[]{:S(2)}) collective-permute-start(f32[256,256]{1,0:T(8,128)S(1)} %get-tuple-element.42.first_slab), channel_id=1, source_target_pairs={{8,0},{16,8},{24,16},{32,24},{40,32},{48,40},{56,48},{64,56},{72,6... | collective-permute-start | bytes 786440 | tf_op jit(solution)/shard_map/ppermute | solution.py:394
  9.5 2.8 %prepare.1 = (f32[2,16,272,128]{3,2,1,0:T(8,128)S(1)}, f32[4,8,128]{2,1,0:T(8,128)S(1)}, f32[4,8,128]{2,1,0:T(8,128)S(1)}, f32[32,8,128]{2,1,0:T(8,128)S(1)}, bf16[128,256]{1,0:T(8,128)(2,1)S(1)}) custom-call(f32[16,256,256]{2,1,0:T(8,128)} %vol.1, f32[256,256]{1,0:T(8,128)S(1)} %get-tuple-element.42.first_slab, f32[256,256]{1,0:T(8,128)S(1)} %get-tuple-element.41.last_slab, ...), custom_call_target="tpu_custom_call" | custom-call | tf_op jit(solution)/shard_map/prepare/pallas_call | solution.py:128
  12.3 1.7 %collective-permute-start.3 = (f32[4,8,128]{2,1,0:T(8,128)S(1)}, f32[4,8,128]{2,1,0:T(8,128)S(1)}, u32[]{:S(2)}, u32[]{:S(2)}) collective-permute-start(f32[4,8,128]{2,1,0:T(8,128)S(1)} %get-tuple-element.27), channel_id=1, source_target_pairs={{1,0},{2,1},{3,2},{4,3},{5,4},{6,5},{7,6},{0,7},{9,8},{10,9},{11,1... | collective-permute-start | bytes 49160 | tf_op jit(solution)/shard_map/ppermute | solution.py:403
  14.1 1.4 %collective-permute-done.2.left = f32[4,8,128]{2,1,0:T(8,128)S(1)} collective-permute-done((f32[4,8,128]{2,1,0:T(8,128)S(1)}, f32[4,8,128]{2,1,0:T(8,128)S(1)}, u32[]{:S(2)}, u32[]{:S(2)}) %collective-permute-start.2) | collective-permute-done | bytes 16416 | tf_op jit(solution)/shard_map/ppermute | solution.py:402
  15.5 0.0 collective-permute-done.3.right
  15.5 0.2 collective-permute-done.low
  15.8 3.3 %away.1.refs_0_ = f32[2,4,4,8,256]{4,3,2,1,0:T(8,128)S(1)} custom-call(f32[32,8,128]{2,1,0:T(8,128)S(1)} %get-tuple-element.23.par, bf16[128,256]{1,0:T(8,128)(2,1)S(1)} %get-tuple-element.24.mix, f32[2,16,272,128]{3,2,1,0:T(8,128)S(1)} %get-tuple-element.25.cells, f32[256,256]{1,0:T(8,128)S(1)} %collective-permute-done.low, ...), custom_call_target="tpu_custom_call" | custom-call | flops 20971520 | bytes 1048576 | tf_op jit(solution)/shard_map/away/pallas_call | solution.py:271
  19.0 0.1 collective-permute-start.4
  19.1 1.6 %near.1.refs_0_ = f32[1,4,4,8,256]{4,3,2,1,0:T(8,128)S(1)} custom-call(f32[32,8,128]{2,1,0:T(8,128)S(1)} %get-tuple-element.23.par, bf16[128,256]{1,0:T(8,128)(2,1)S(1)} %get-tuple-element.24.mix, f32[2,16,272,128]{3,2,1,0:T(8,128)S(1)} %get-tuple-element.25.cells, f32[256,256]{1,0:T(8,128)S(1)} %collective-permute-done.low, ...), custom_call_target="tpu_custom_call" | custom-call | flops 10485760 | bytes 524288 | tf_op jit(solution)/shard_map/near/pallas_call | solution.py:271
  20.8 1.5 %collective-permute-start.6 = (f32[1,4,4,8,256]{4,3,2,1,0:T(8,128)S(1)}, f32[1,4,4,8,256]{4,3,2,1,0:T(8,128)S(1)}, u32[]{:S(2)}, u32[]{:S(2)}) collective-permute-start(f32[1,4,4,8,256]{4,3,2,1,0:T(8,128)S(1)} %near.1.refs_0_), channel_id=1, source_target_pairs={{0,56},{8,16},{16,8},{24,32},{32,24},{40,48},{48,40},{56,0},{64,12... | collective-permute-start | bytes 393224 | tf_op jit(solution)/shard_map/ppermute | solution.py:406
  22.2 1.7 %past.1.refs_1_ = f32[1,4,4,8,256]{4,3,2,1,0:T(8,128)S(1)} custom-call(f32[32,8,128]{2,1,0:T(8,128)S(1)} %get-tuple-element.23.par, bf16[128,256]{1,0:T(8,128)(2,1)S(1)} %get-tuple-element.24.mix, f32[2,16,272,128]{3,2,1,0:T(8,128)S(1)} %get-tuple-element.25.cells, f32[256,256]{1,0:T(8,128)S(1)} %collective-permute-done.low, ...), custom_call_target="tpu_custom_call" | custom-call | flops 10485760 | bytes 524288 | tf_op jit(solution)/shard_map/past/pallas_call | solution.py:271
  23.9 2.1 %collective-permute-start.7 = (f32[1,4,4,8,256]{4,3,2,1,0:T(8,128)S(1)}, f32[1,4,4,8,256]{4,3,2,1,0:T(8,128)S(1)}, u32[]{:S(2)}, u32[]{:S(2)}) collective-permute-start(f32[1,4,4,8,256]{4,3,2,1,0:T(8,128)S(1)} %past.1.refs_1_), channel_id=1, source_target_pairs={{0,16},{8,56},{16,32},{24,8},{32,48},{40,24},{48,0},{56,40},{64,80... | collective-permute-start | bytes 393224 | tf_op jit(solution)/shard_map/ppermute | solution.py:406
  26.0 2.2 %collective-permute-done.4.refs_0_ = f32[2,4,4,8,256]{4,3,2,1,0:T(8,128)S(1)} collective-permute-done((f32[2,4,4,8,256]{4,3,2,1,0:T(8,128)S(1)}, f32[2,4,4,8,256]{4,3,2,1,0:T(8,128)S(1)}, u32[]{:S(2)}, u32[]{:S(2)}) %collective-permute-start.4) | collective-permute-done | bytes 262176 | tf_op jit(solution)/shard_map/ppermute | solution.py:406
  28.2 1.7 %keep3.1.refs_1_ = f32[1,4,4,8,256]{4,3,2,1,0:T(8,128)S(1)} custom-call(f32[32,8,128]{2,1,0:T(8,128)S(1)} %get-tuple-element.23.par, bf16[128,256]{1,0:T(8,128)(2,1)S(1)} %get-tuple-element.24.mix, f32[2,16,272,128]{3,2,1,0:T(8,128)S(1)} %get-tuple-element.25.cells, f32[256,256]{1,0:T(8,128)S(1)} %collective-permute-done.low, ...), custom_call_target="tpu_custom_call" | custom-call | flops 10485760 | bytes 524288 | tf_op jit(solution)/shard_map/keep3/pallas_call | solution.py:271
  29.9 1.1 %collective-permute-start.8 = (f32[1,4,4,8,256]{4,3,2,1,0:T(8,128)S(1)}, f32[1,4,4,8,256]{4,3,2,1,0:T(8,128)S(1)}, u32[]{:S(2)}, u32[]{:S(2)}) collective-permute-start(f32[1,4,4,8,256]{4,3,2,1,0:T(8,128)S(1)} %keep3.1.refs_1_), channel_id=1, source_target_pairs={{0,40},{8,32},{16,56},{24,48},{32,8},{40,0},{48,24},{56,16},{64,10... | collective-permute-start | bytes 393224 | tf_op jit(solution)/shard_map/ppermute | solution.py:406
  31.0 1.7 %keep2.1.refs_0_ = f32[1,4,4,8,256]{4,3,2,1,0:T(8,128)S(1)} custom-call(f32[32,8,128]{2,1,0:T(8,128)S(1)} %get-tuple-element.23.par, bf16[128,256]{1,0:T(8,128)(2,1)S(1)} %get-tuple-element.24.mix, f32[2,16,272,128]{3,2,1,0:T(8,128)S(1)} %get-tuple-element.25.cells, f32[256,256]{1,0:T(8,128)S(1)} %collective-permute-done.low, ...), custom_call_target="tpu_custom_call" | custom-call | flops 10485760 | bytes 524288 | tf_op jit(solution)/shard_map/keep2/pallas_call | solution.py:271
  32.7 1.6 %collective-permute-start.9 = (f32[1,4,4,8,256]{4,3,2,1,0:T(8,128)S(1)}, f32[1,4,4,8,256]{4,3,2,1,0:T(8,128)S(1)}, u32[]{:S(2)}, u32[]{:S(2)}) collective-permute-start(f32[1,4,4,8,256]{4,3,2,1,0:T(8,128)S(1)} %keep2.1.refs_0_), channel_id=1, source_target_pairs={{0,48},{8,24},{16,0},{24,40},{32,16},{40,56},{48,32},{56,8},{64,11... | collective-permute-start | bytes 393224 | tf_op jit(solution)/shard_map/ppermute | solution.py:406
  34.3 1.6 %mate.1.refs_0_ = f32[1,4,4,8,256]{4,3,2,1,0:T(8,128)S(1)} custom-call(f32[32,8,128]{2,1,0:T(8,128)S(1)} %get-tuple-element.23.par, bf16[128,256]{1,0:T(8,128)(2,1)S(1)} %get-tuple-element.24.mix, f32[2,16,272,128]{3,2,1,0:T(8,128)S(1)} %get-tuple-element.25.cells, f32[256,256]{1,0:T(8,128)S(1)} %collective-permute-done.low, ...), custom_call_target="tpu_custom_call" | custom-call | flops 10485760 | bytes 524288 | tf_op jit(solution)/shard_map/mate/pallas_call | solution.py:271
  35.9 0.7 %collective-permute-start.5 = (f32[1,4,4,8,256]{4,3,2,1,0:T(8,128)S(1)}, f32[1,4,4,8,256]{4,3,2,1,0:T(8,128)S(1)}, u32[]{:S(2)}, u32[]{:S(2)}) collective-permute-start(f32[1,4,4,8,256]{4,3,2,1,0:T(8,128)S(1)} %mate.1.refs_0_), channel_id=1, source_target_pairs={{0,8},{8,0},{16,24},{24,16},{32,40},{40,32},{48,56},{56,48},{64,72... | collective-permute-start | bytes 393224 | tf_op jit(solution)/shard_map/ppermute | solution.py:406
  36.7 1.6 %own.1.refs_0_ = f32[1,4,4,8,256]{4,3,2,1,0:T(8,128)S(1)} custom-call(f32[32,8,128]{2,1,0:T(8,128)S(1)} %get-tuple-element.23.par, bf16[128,256]{1,0:T(8,128)(2,1)S(1)} %get-tuple-element.24.mix, f32[2,16,272,128]{3,2,1,0:T(8,128)S(1)} %get-tuple-element.25.cells, f32[256,256]{1,0:T(8,128)S(1)} %collective-permute-done.low, ...), custom_call_target="tpu_custom_call" | custom-call | flops 10485760 | bytes 524288 | tf_op jit(solution)/shard_map/own/pallas_call | solution.py:271
  38.3 2.1 %collective-permute-done.8.refs_2_ = f32[1,4,4,8,256]{4,3,2,1,0:T(8,128)S(1)} collective-permute-done((f32[1,4,4,8,256]{4,3,2,1,0:T(8,128)S(1)}, f32[1,4,4,8,256]{4,3,2,1,0:T(8,128)S(1)}, u32[]{:S(2)}, u32[]{:S(2)}) %collective-permute-start.8) | collective-permute-done | bytes 131104 | tf_op jit(solution)/shard_map/ppermute | solution.py:406
  40.4 1.2 %collective-permute-done.9.refs_3_ = f32[1,4,4,8,256]{4,3,2,1,0:T(8,128)S(1)} collective-permute-done((f32[1,4,4,8,256]{4,3,2,1,0:T(8,128)S(1)}, f32[1,4,4,8,256]{4,3,2,1,0:T(8,128)S(1)}, u32[]{:S(2)}, u32[]{:S(2)}) %collective-permute-start.9) | collective-permute-done | bytes 131104 | tf_op jit(solution)/shard_map/ppermute | solution.py:406
  41.6 1.0 %collective-permute-done.5.refs_1_ = f32[1,4,4,8,256]{4,3,2,1,0:T(8,128)S(1)} collective-permute-done((f32[1,4,4,8,256]{4,3,2,1,0:T(8,128)S(1)}, f32[1,4,4,8,256]{4,3,2,1,0:T(8,128)S(1)}, u32[]{:S(2)}, u32[]{:S(2)}) %collective-permute-start.5) | collective-permute-done | bytes 131104 | tf_op jit(solution)/shard_map/ppermute | solution.py:406
  42.6 0.1 merge_z.1
  42.7 1.5 %collective-permute-start.10 = (f32[4,8,256]{2,1,0:T(8,128)S(1)}, f32[4,8,256]{2,1,0:T(8,128)S(1)}, u32[]{:S(2)}, u32[]{:S(2)}) collective-permute-start(f32[4,8,256]{2,1,0:T(8,128)S(1)} %get-tuple-element.38), channel_id=1, source_target_pairs={{0,64},{8,72},{16,80},{24,88},{32,96},{40,104},{48,112},{56,120},{... | collective-permute-start | bytes 98312 | tf_op jit(solution)/shard_map/ppermute | solution.py:439
  44.1 2.3 %collective-permute-start.11 = (f32[4,8,256]{2,1,0:T(8,128)S(1)}, f32[4,8,256]{2,1,0:T(8,128)S(1)}, u32[]{:S(2)}, u32[]{:S(2)}) collective-permute-start(f32[4,8,256]{2,1,0:T(8,128)S(1)} %get-tuple-element.39), channel_id=1, source_target_pairs={{0,128},{8,136},{16,144},{24,152},{32,160},{40,168},{48,176},{56,1... | collective-permute-start | bytes 98312 | tf_op jit(solution)/shard_map/ppermute | solution.py:439
  46.5 1.9 %collective-permute-start.12 = (f32[4,8,256]{2,1,0:T(8,128)S(1)}, f32[4,8,256]{2,1,0:T(8,128)S(1)}, u32[]{:S(2)}, u32[]{:S(2)}) collective-permute-start(f32[4,8,256]{2,1,0:T(8,128)S(1)} %get-tuple-element.40), channel_id=1, source_target_pairs={{0,192},{8,200},{16,208},{24,216},{32,224},{40,232},{48,240},{56,2... | collective-permute-start | bytes 98312 | tf_op jit(solution)/shard_map/ppermute | solution.py:439
  48.3 1.2 %collective-permute-done.11.refs_2_ = f32[4,8,256]{2,1,0:T(8,128)S(1)} collective-permute-done((f32[4,8,256]{2,1,0:T(8,128)S(1)}, f32[4,8,256]{2,1,0:T(8,128)S(1)}, u32[]{:S(2)}, u32[]{:S(2)}) %collective-permute-start.11) | collective-permute-done | bytes 32800 | tf_op jit(solution)/shard_map/ppermute | solution.py:439
  49.6 0.8 %collective-permute-done.12.refs_3_ = f32[4,8,256]{2,1,0:T(8,128)S(1)} collective-permute-done((f32[4,8,256]{2,1,0:T(8,128)S(1)}, f32[4,8,256]{2,1,0:T(8,128)S(1)}, u32[]{:S(2)}, u32[]{:S(2)}) %collective-permute-start.12) | collective-permute-done | bytes 32800 | tf_op jit(solution)/shard_map/ppermute | solution.py:439
  50.4 0.6 %merge_y.1 = f32[4,8,256]{2,1,0:T(8,128)} custom-call(f32[4,8,256]{2,1,0:T(8,128)S(1)} %get-tuple-element.37.refs_0_, f32[4,8,256]{2,1,0:T(8,128)S(1)} %collective-permute-done.10.refs_1_, f32[4,8,256]{2,1,0:T(8,128)S(1)} %collective-permute-done.11.refs_2_, f32[4,8,256]{2,1,0:T(8,128)S(1)} %collective-permute-done.12.refs_3_), custom_call_target="tpu_custom_call" | custom-call | tf_op jit(solution)/shard_map/merge_y/pallas_call | solution.py:371
  (9 shorter events, 0.0 us)
Async XLA Ops:
  1.1 14.7 %collective-permute-start = (f32[256,256]{1,0:T(8,128)S(1)}, f32[256,256]{1,0:T(8,128)S(1)}, u32[]{:S(2)}, u32[]{:S(2)}) collective-permute-start(f32[256,256]{1,0:T(8,128)S(1)} %get-tuple-element.41.last_slab), channel_id=1, source_target_pairs={{0,8},{8,16},{16,24},{24,32},{32,40},{40,48},{48,56},{56,64},{64,7... | collective-permute-start | bytes 786440 | tf_op jit(solution)/shard_map/ppermute | solution.py:393
  3.1 12.7 %collective-permute-start.1 = (f32[256,256]{1,0:T(8,128)S(1)}, f32[256,256]{1,0:T(8,128)S(1)}, u32[]{:S(2)}, u32[]{:S(2)}) collective-permute-start(f32[256,256]{1,0:T(8,128)S(1)} %get-tuple-element.42.first_slab), channel_id=1, source_target_pairs={{8,0},{16,8},{24,16},{32,24},{40,32},{48,40},{56,48},{64,56},{72,6... | collective-permute-start | bytes 786440 | tf_op jit(solution)/shard_map/ppermute | solution.py:394
  12.3 3.2 %collective-permute-start.2 = (f32[4,8,128]{2,1,0:T(8,128)S(1)}, f32[4,8,128]{2,1,0:T(8,128)S(1)}, u32[]{:S(2)}, u32[]{:S(2)}) collective-permute-start(f32[4,8,128]{2,1,0:T(8,128)S(1)} %get-tuple-element.26), channel_id=1, source_target_pairs={{0,1},{1,2},{2,3},{3,4},{4,5},{5,6},{6,7},{7,0},{8,9},{9,10},{10,1... | collective-permute-start | bytes 49160 | tf_op jit(solution)/shard_map/ppermute | solution.py:402
  12.3 3.2 %collective-permute-start.3 = (f32[4,8,128]{2,1,0:T(8,128)S(1)}, f32[4,8,128]{2,1,0:T(8,128)S(1)}, u32[]{:S(2)}, u32[]{:S(2)}) collective-permute-start(f32[4,8,128]{2,1,0:T(8,128)S(1)} %get-tuple-element.27), channel_id=1, source_target_pairs={{1,0},{2,1},{3,2},{4,3},{5,4},{6,5},{7,6},{0,7},{9,8},{10,9},{11,1... | collective-permute-start | bytes 49160 | tf_op jit(solution)/shard_map/ppermute | solution.py:403
  19.0 9.2 %collective-permute-start.4 = (f32[2,4,4,8,256]{4,3,2,1,0:T(8,128)S(1)}, f32[2,4,4,8,256]{4,3,2,1,0:T(8,128)S(1)}, u32[]{:S(2)}, u32[]{:S(2)}) collective-permute-start(f32[2,4,4,8,256]{4,3,2,1,0:T(8,128)S(1)} %away.1.refs_0_), channel_id=1, source_target_pairs={{0,8},{8,0},{16,24},{24,16},{32,40},{40,32},{48,56},{56,48},{64,72... | collective-permute-start | bytes 786440 | tf_op jit(solution)/shard_map/ppermute | solution.py:406
  20.8 15.9 %collective-permute-start.6 = (f32[1,4,4,8,256]{4,3,2,1,0:T(8,128)S(1)}, f32[1,4,4,8,256]{4,3,2,1,0:T(8,128)S(1)}, u32[]{:S(2)}, u32[]{:S(2)}) collective-permute-start(f32[1,4,4,8,256]{4,3,2,1,0:T(8,128)S(1)} %near.1.refs_0_), channel_id=1, source_target_pairs={{0,56},{8,16},{16,8},{24,32},{32,24},{40,48},{48,40},{56,0},{64,12... | collective-permute-start | bytes 393224 | tf_op jit(solution)/shard_map/ppermute | solution.py:406
  23.9 12.7 %collective-permute-start.7 = (f32[1,4,4,8,256]{4,3,2,1,0:T(8,128)S(1)}, f32[1,4,4,8,256]{4,3,2,1,0:T(8,128)S(1)}, u32[]{:S(2)}, u32[]{:S(2)}) collective-permute-start(f32[1,4,4,8,256]{4,3,2,1,0:T(8,128)S(1)} %past.1.refs_1_), channel_id=1, source_target_pairs={{0,16},{8,56},{16,32},{24,8},{32,48},{40,24},{48,0},{56,40},{64,80... | collective-permute-start | bytes 393224 | tf_op jit(solution)/shard_map/ppermute | solution.py:406
  29.9 10.5 %collective-permute-start.8 = (f32[1,4,4,8,256]{4,3,2,1,0:T(8,128)S(1)}, f32[1,4,4,8,256]{4,3,2,1,0:T(8,128)S(1)}, u32[]{:S(2)}, u32[]{:S(2)}) collective-permute-start(f32[1,4,4,8,256]{4,3,2,1,0:T(8,128)S(1)} %keep3.1.refs_1_), channel_id=1, source_target_pairs={{0,40},{8,32},{16,56},{24,48},{32,8},{40,0},{48,24},{56,16},{64,10... | collective-permute-start | bytes 393224 | tf_op jit(solution)/shard_map/ppermute | solution.py:406
  32.7 8.9 %collective-permute-start.9 = (f32[1,4,4,8,256]{4,3,2,1,0:T(8,128)S(1)}, f32[1,4,4,8,256]{4,3,2,1,0:T(8,128)S(1)}, u32[]{:S(2)}, u32[]{:S(2)}) collective-permute-start(f32[1,4,4,8,256]{4,3,2,1,0:T(8,128)S(1)} %keep2.1.refs_0_), channel_id=1, source_target_pairs={{0,48},{8,24},{16,0},{24,40},{32,16},{40,56},{48,32},{56,8},{64,11... | collective-permute-start | bytes 393224 | tf_op jit(solution)/shard_map/ppermute | solution.py:406
  35.9 6.6 %collective-permute-start.5 = (f32[1,4,4,8,256]{4,3,2,1,0:T(8,128)S(1)}, f32[1,4,4,8,256]{4,3,2,1,0:T(8,128)S(1)}, u32[]{:S(2)}, u32[]{:S(2)}) collective-permute-start(f32[1,4,4,8,256]{4,3,2,1,0:T(8,128)S(1)} %mate.1.refs_0_), channel_id=1, source_target_pairs={{0,8},{8,0},{16,24},{24,16},{32,40},{40,32},{48,56},{56,48},{64,72... | collective-permute-start | bytes 393224 | tf_op jit(solution)/shard_map/ppermute | solution.py:406
  42.7 5.7 %collective-permute-start.10 = (f32[4,8,256]{2,1,0:T(8,128)S(1)}, f32[4,8,256]{2,1,0:T(8,128)S(1)}, u32[]{:S(2)}, u32[]{:S(2)}) collective-permute-start(f32[4,8,256]{2,1,0:T(8,128)S(1)} %get-tuple-element.38), channel_id=1, source_target_pairs={{0,64},{8,72},{16,80},{24,88},{32,96},{40,104},{48,112},{56,120},{... | collective-permute-start | bytes 98312 | tf_op jit(solution)/shard_map/ppermute | solution.py:439
  44.1 5.4 %collective-permute-start.11 = (f32[4,8,256]{2,1,0:T(8,128)S(1)}, f32[4,8,256]{2,1,0:T(8,128)S(1)}, u32[]{:S(2)}, u32[]{:S(2)}) collective-permute-start(f32[4,8,256]{2,1,0:T(8,128)S(1)} %get-tuple-element.39), channel_id=1, source_target_pairs={{0,128},{8,136},{16,144},{24,152},{32,160},{40,168},{48,176},{56,1... | collective-permute-start | bytes 98312 | tf_op jit(solution)/shard_map/ppermute | solution.py:439
  46.5 3.9 %collective-permute-start.12 = (f32[4,8,256]{2,1,0:T(8,128)S(1)}, f32[4,8,256]{2,1,0:T(8,128)S(1)}, u32[]{:S(2)}, u32[]{:S(2)}) collective-permute-start(f32[4,8,256]{2,1,0:T(8,128)S(1)} %get-tuple-element.40), channel_id=1, source_target_pairs={{0,192},{8,200},{16,208},{24,216},{32,224},{40,232},{48,240},{56,2... | collective-permute-start | bytes 98312 | tf_op jit(solution)/shard_map/ppermute | solution.py:439

commit v5 on v4

--- a/solution.py
+++ b/solution.py
@@ -13,7 +13,7 @@
 BUMPS = 8
 LIMIT = 16 * 1024 * 1024
 MIX = 256
-BODY = 2
+BODY = 4
 VMEM = pl.BlockSpec(memory_space=pltpu.VMEM)
 
 

time: 51.8 us -> 51.9 us (level)
  no operation moved by 1% of the time
where the time goes in v5:
time: 51.9 us; the launch traced here: 51.1 us
  starting transfers between devices  23.3 us (45%)
  Pallas kernels  16.5 us (32%)
  waiting for transfers between devices  10.2 us (20%)
  local copies, waits for them, and re-layouts  1.06 us (2%)
    pallas_call x7, Pallas kernels, march(): pl.pallas_call(functools.partial(march_kernel, away, slot, len(after), ne...  12.9 us
    ppermute x6, starting transfers between devices, along_z(): lax.ppermute(x, 'depth', [(y * zs + z, y * zs + to(z) % zs) for y in rang...  7.11 us
    ppermute x1, starting transfers between devices, on_device(): high = lax.ppermute(first_slab, 'depth', down)  6.48 us
    ppermute x6, waiting for transfers between devices, along_z(): lax.ppermute(x, 'depth', [(y * zs + z, y * zs + to(z) % zs) for y in rang...  6.45 us
    ppermute x3, starting transfers between devices, on_device(): merged[t] = lax.ppermute(merged[t], 'depth', pairs)  5.97 us
    pallas_call x1, Pallas kernels, prepare(): pl.pallas_call(functools.partial(prepare_kernel, depth_all), out_shape=(j...  2.77 us
    ppermute x3, waiting for transfers between devices, on_device(): merged[t] = lax.ppermute(merged[t], 'depth', pairs)  2.09 us
    ppermute x1, starting transfers between devices, on_device(): low = lax.ppermute(last_slab, 'depth', up)  1.99 us
  transfers between devices with their start and end apart: 13, of which 8 were waited for; matrix products, arithmetic and copies ran while one was open for 0% of the time, Pallas kernels for 25%

profile of v5, /device:TPU:4, one launch (start us, length us, event | category | flops | bytes accessed | tf_op | source)
XLA Modules:
  0.0 51.1 jit_solution(11200283404144783122)
XLA Ops:
  0.0 1.1 %slice_bitcast_fusion = (f32[256,256]{1,0:T(8,128)S(1)}, f32[256,256]{1,0:T(8,128)S(1)}) fusion(f32[16,256,256]{2,1,0:T(8,128)} %vol.1), kind=kLoop, calls=%fused_computation | loop fusion | bytes 1048576 | tf_op jit(solution)/shard_map/squeeze | solution.py:392
  1.1 2.0 %collective-permute-start = (f32[256,256]{1,0:T(8,128)S(1)}, f32[256,256]{1,0:T(8,128)S(1)}, u32[]{:S(2)}, u32[]{:S(2)}) collective-permute-start(f32[256,256]{1,0:T(8,128)S(1)} %get-tuple-element.41.last_slab), channel_id=1, source_target_pairs={{0,8},{8,16},{16,24},{24,32},{32,40},{40,48},{48,56},{56,64},{64,7... | collective-permute-start | bytes 786440 | tf_op jit(solution)/shard_map/ppermute | solution.py:393
  3.1 6.5 %collective-permute-start.1 = (f32[256,256]{1,0:T(8,128)S(1)}, f32[256,256]{1,0:T(8,128)S(1)}, u32[]{:S(2)}, u32[]{:S(2)}) collective-permute-start(f32[256,256]{1,0:T(8,128)S(1)} %get-tuple-element.42.first_slab), channel_id=1, source_target_pairs={{8,0},{16,8},{24,16},{32,24},{40,32},{48,40},{56,48},{64,56},{72,6... | collective-permute-start | bytes 786440 | tf_op jit(solution)/shard_map/ppermute | solution.py:394
  9.5 2.8 %prepare.1 = (f32[2,16,272,128]{3,2,1,0:T(8,128)S(1)}, f32[4,8,128]{2,1,0:T(8,128)S(1)}, f32[4,8,128]{2,1,0:T(8,128)S(1)}, f32[32,8,128]{2,1,0:T(8,128)S(1)}, bf16[128,256]{1,0:T(8,128)(2,1)S(1)}) custom-call(f32[16,256,256]{2,1,0:T(8,128)} %vol.1, f32[256,256]{1,0:T(8,128)S(1)} %get-tuple-element.42.first_slab, f32[256,256]{1,0:T(8,128)S(1)} %get-tuple-element.41.last_slab, ...), custom_call_target="tpu_custom_call" | custom-call | tf_op jit(solution)/shard_map/prepare/pallas_call | solution.py:128
  12.3 1.7 %collective-permute-start.3 = (f32[4,8,128]{2,1,0:T(8,128)S(1)}, f32[4,8,128]{2,1,0:T(8,128)S(1)}, u32[]{:S(2)}, u32[]{:S(2)}) collective-permute-start(f32[4,8,128]{2,1,0:T(8,128)S(1)} %get-tuple-element.27), channel_id=1, source_target_pairs={{1,0},{2,1},{3,2},{4,3},{5,4},{6,5},{7,6},{0,7},{9,8},{10,9},{11,1... | collective-permute-start | bytes 49160 | tf_op jit(solution)/shard_map/ppermute | solution.py:403
  14.1 1.4 %collective-permute-done.2.left = f32[4,8,128]{2,1,0:T(8,128)S(1)} collective-permute-done((f32[4,8,128]{2,1,0:T(8,128)S(1)}, f32[4,8,128]{2,1,0:T(8,128)S(1)}, u32[]{:S(2)}, u32[]{:S(2)}) %collective-permute-start.2) | collective-permute-done | bytes 16416 | tf_op jit(solution)/shard_map/ppermute | solution.py:402
  15.5 0.0 collective-permute-done.3.right
  15.5 0.2 collective-permute-done.low
  15.8 3.2 %away.1.refs_0_ = f32[2,4,4,8,256]{4,3,2,1,0:T(8,128)S(1)} custom-call(f32[32,8,128]{2,1,0:T(8,128)S(1)} %get-tuple-element.23.par, bf16[128,256]{1,0:T(8,128)(2,1)S(1)} %get-tuple-element.24.mix, f32[2,16,272,128]{3,2,1,0:T(8,128)S(1)} %get-tuple-element.25.cells, f32[256,256]{1,0:T(8,128)S(1)} %collective-permute-done.low, ...), custom_call_target="tpu_custom_call" | custom-call | flops 20971520 | bytes 1048576 | tf_op jit(solution)/shard_map/away/pallas_call | solution.py:271
  18.9 0.1 collective-permute-start.4
  19.0 1.6 %near.1.refs_0_ = f32[1,4,4,8,256]{4,3,2,1,0:T(8,128)S(1)} custom-call(f32[32,8,128]{2,1,0:T(8,128)S(1)} %get-tuple-element.23.par, bf16[128,256]{1,0:T(8,128)(2,1)S(1)} %get-tuple-element.24.mix, f32[2,16,272,128]{3,2,1,0:T(8,128)S(1)} %get-tuple-element.25.cells, f32[256,256]{1,0:T(8,128)S(1)} %collective-permute-done.low, ...), custom_call_target="tpu_custom_call" | custom-call | flops 10485760 | bytes 524288 | tf_op jit(solution)/shard_map/near/pallas_call | solution.py:271
  20.7 1.5 %collective-permute-start.6 = (f32[1,4,4,8,256]{4,3,2,1,0:T(8,128)S(1)}, f32[1,4,4,8,256]{4,3,2,1,0:T(8,128)S(1)}, u32[]{:S(2)}, u32[]{:S(2)}) collective-permute-start(f32[1,4,4,8,256]{4,3,2,1,0:T(8,128)S(1)} %near.1.refs_0_), channel_id=1, source_target_pairs={{0,56},{8,16},{16,8},{24,32},{32,24},{40,48},{48,40},{56,0},{64,12... | collective-permute-start | bytes 393224 | tf_op jit(solution)/shard_map/ppermute | solution.py:406
  22.1 1.7 %past.1.refs_1_ = f32[1,4,4,8,256]{4,3,2,1,0:T(8,128)S(1)} custom-call(f32[32,8,128]{2,1,0:T(8,128)S(1)} %get-tuple-element.23.par, bf16[128,256]{1,0:T(8,128)(2,1)S(1)} %get-tuple-element.24.mix, f32[2,16,272,128]{3,2,1,0:T(8,128)S(1)} %get-tuple-element.25.cells, f32[256,256]{1,0:T(8,128)S(1)} %collective-permute-done.low, ...), custom_call_target="tpu_custom_call" | custom-call | flops 10485760 | bytes 524288 | tf_op jit(solution)/shard_map/past/pallas_call | solution.py:271
  23.8 2.1 %collective-permute-start.7 = (f32[1,4,4,8,256]{4,3,2,1,0:T(8,128)S(1)}, f32[1,4,4,8,256]{4,3,2,1,0:T(8,128)S(1)}, u32[]{:S(2)}, u32[]{:S(2)}) collective-permute-start(f32[1,4,4,8,256]{4,3,2,1,0:T(8,128)S(1)} %past.1.refs_1_), channel_id=1, source_target_pairs={{0,16},{8,56},{16,32},{24,8},{32,48},{40,24},{48,0},{56,40},{64,80... | collective-permute-start | bytes 393224 | tf_op jit(solution)/shard_map/ppermute | solution.py:406
  25.9 2.2 %collective-permute-done.4.refs_0_ = f32[2,4,4,8,256]{4,3,2,1,0:T(8,128)S(1)} collective-permute-done((f32[2,4,4,8,256]{4,3,2,1,0:T(8,128)S(1)}, f32[2,4,4,8,256]{4,3,2,1,0:T(8,128)S(1)}, u32[]{:S(2)}, u32[]{:S(2)}) %collective-permute-start.4) | collective-permute-done | bytes 262176 | tf_op jit(solution)/shard_map/ppermute | solution.py:406
  28.1 1.6 %keep3.1.refs_1_ = f32[1,4,4,8,256]{4,3,2,1,0:T(8,128)S(1)} custom-call(f32[32,8,128]{2,1,0:T(8,128)S(1)} %get-tuple-element.23.par, bf16[128,256]{1,0:T(8,128)(2,1)S(1)} %get-tuple-element.24.mix, f32[2,16,272,128]{3,2,1,0:T(8,128)S(1)} %get-tuple-element.25.cells, f32[256,256]{1,0:T(8,128)S(1)} %collective-permute-done.low, ...), custom_call_target="tpu_custom_call" | custom-call | flops 10485760 | bytes 524288 | tf_op jit(solution)/shard_map/keep3/pallas_call | solution.py:271
  29.8 1.2 %collective-permute-start.8 = (f32[1,4,4,8,256]{4,3,2,1,0:T(8,128)S(1)}, f32[1,4,4,8,256]{4,3,2,1,0:T(8,128)S(1)}, u32[]{:S(2)}, u32[]{:S(2)}) collective-permute-start(f32[1,4,4,8,256]{4,3,2,1,0:T(8,128)S(1)} %keep3.1.refs_1_), channel_id=1, source_target_pairs={{0,40},{8,32},{16,56},{24,48},{32,8},{40,0},{48,24},{56,16},{64,10... | collective-permute-start | bytes 393224 | tf_op jit(solution)/shard_map/ppermute | solution.py:406
  31.0 1.7 %keep2.1.refs_0_ = f32[1,4,4,8,256]{4,3,2,1,0:T(8,128)S(1)} custom-call(f32[32,8,128]{2,1,0:T(8,128)S(1)} %get-tuple-element.23.par, bf16[128,256]{1,0:T(8,128)(2,1)S(1)} %get-tuple-element.24.mix, f32[2,16,272,128]{3,2,1,0:T(8,128)S(1)} %get-tuple-element.25.cells, f32[256,256]{1,0:T(8,128)S(1)} %collective-permute-done.low, ...), custom_call_target="tpu_custom_call" | custom-call | flops 10485760 | bytes 524288 | tf_op jit(solution)/shard_map/keep2/pallas_call | solution.py:271
  32.7 1.6 %collective-permute-start.9 = (f32[1,4,4,8,256]{4,3,2,1,0:T(8,128)S(1)}, f32[1,4,4,8,256]{4,3,2,1,0:T(8,128)S(1)}, u32[]{:S(2)}, u32[]{:S(2)}) collective-permute-start(f32[1,4,4,8,256]{4,3,2,1,0:T(8,128)S(1)} %keep2.1.refs_0_), channel_id=1, source_target_pairs={{0,48},{8,24},{16,0},{24,40},{32,16},{40,56},{48,32},{56,8},{64,11... | collective-permute-start | bytes 393224 | tf_op jit(solution)/shard_map/ppermute | solution.py:406
  34.2 1.6 %mate.1.refs_0_ = f32[1,4,4,8,256]{4,3,2,1,0:T(8,128)S(1)} custom-call(f32[32,8,128]{2,1,0:T(8,128)S(1)} %get-tuple-element.23.par, bf16[128,256]{1,0:T(8,128)(2,1)S(1)} %get-tuple-element.24.mix, f32[2,16,272,128]{3,2,1,0:T(8,128)S(1)} %get-tuple-element.25.cells, f32[256,256]{1,0:T(8,128)S(1)} %collective-permute-done.low, ...), custom_call_target="tpu_custom_call" | custom-call | flops 10485760 | bytes 524288 | tf_op jit(solution)/shard_map/mate/pallas_call | solution.py:271
  35.9 0.7 %collective-permute-start.5 = (f32[1,4,4,8,256]{4,3,2,1,0:T(8,128)S(1)}, f32[1,4,4,8,256]{4,3,2,1,0:T(8,128)S(1)}, u32[]{:S(2)}, u32[]{:S(2)}) collective-permute-start(f32[1,4,4,8,256]{4,3,2,1,0:T(8,128)S(1)} %mate.1.refs_0_), channel_id=1, source_target_pairs={{0,8},{8,0},{16,24},{24,16},{32,40},{40,32},{48,56},{56,48},{64,72... | collective-permute-start | bytes 393224 | tf_op jit(solution)/shard_map/ppermute | solution.py:406
  36.5 1.5 %own.1.refs_0_ = f32[1,4,4,8,256]{4,3,2,1,0:T(8,128)S(1)} custom-call(f32[32,8,128]{2,1,0:T(8,128)S(1)} %get-tuple-element.23.par, bf16[128,256]{1,0:T(8,128)(2,1)S(1)} %get-tuple-element.24.mix, f32[2,16,272,128]{3,2,1,0:T(8,128)S(1)} %get-tuple-element.25.cells, f32[256,256]{1,0:T(8,128)S(1)} %collective-permute-done.low, ...), custom_call_target="tpu_custom_call" | custom-call | flops 10485760 | bytes 524288 | tf_op jit(solution)/shard_map/own/pallas_call | solution.py:271
  38.1 2.4 %collective-permute-done.8.refs_2_ = f32[1,4,4,8,256]{4,3,2,1,0:T(8,128)S(1)} collective-permute-done((f32[1,4,4,8,256]{4,3,2,1,0:T(8,128)S(1)}, f32[1,4,4,8,256]{4,3,2,1,0:T(8,128)S(1)}, u32[]{:S(2)}, u32[]{:S(2)}) %collective-permute-start.8) | collective-permute-done | bytes 131104 | tf_op jit(solution)/shard_map/ppermute | solution.py:406
  40.5 1.1 %collective-permute-done.9.refs_3_ = f32[1,4,4,8,256]{4,3,2,1,0:T(8,128)S(1)} collective-permute-done((f32[1,4,4,8,256]{4,3,2,1,0:T(8,128)S(1)}, f32[1,4,4,8,256]{4,3,2,1,0:T(8,128)S(1)}, u32[]{:S(2)}, u32[]{:S(2)}) %collective-permute-start.9) | collective-permute-done | bytes 131104 | tf_op jit(solution)/shard_map/ppermute | solution.py:406
  41.6 0.7 %collective-permute-done.5.refs_1_ = f32[1,4,4,8,256]{4,3,2,1,0:T(8,128)S(1)} collective-permute-done((f32[1,4,4,8,256]{4,3,2,1,0:T(8,128)S(1)}, f32[1,4,4,8,256]{4,3,2,1,0:T(8,128)S(1)}, u32[]{:S(2)}, u32[]{:S(2)}) %collective-permute-start.5) | collective-permute-done | bytes 131104 | tf_op jit(solution)/shard_map/ppermute | solution.py:406
  42.3 0.1 merge_z.1
  42.4 1.7 %collective-permute-start.10 = (f32[4,8,256]{2,1,0:T(8,128)S(1)}, f32[4,8,256]{2,1,0:T(8,128)S(1)}, u32[]{:S(2)}, u32[]{:S(2)}) collective-permute-start(f32[4,8,256]{2,1,0:T(8,128)S(1)} %get-tuple-element.38), channel_id=1, source_target_pairs={{0,64},{8,72},{16,80},{24,88},{32,96},{40,104},{48,112},{56,120},{... | collective-permute-start | bytes 98312 | tf_op jit(solution)/shard_map/ppermute | solution.py:439
  44.2 2.4 %collective-permute-start.11 = (f32[4,8,256]{2,1,0:T(8,128)S(1)}, f32[4,8,256]{2,1,0:T(8,128)S(1)}, u32[]{:S(2)}, u32[]{:S(2)}) collective-permute-start(f32[4,8,256]{2,1,0:T(8,128)S(1)} %get-tuple-element.39), channel_id=1, source_target_pairs={{0,128},{8,136},{16,144},{24,152},{32,160},{40,168},{48,176},{56,1... | collective-permute-start | bytes 98312 | tf_op jit(solution)/shard_map/ppermute | solution.py:439
  46.6 1.8 %collective-permute-start.12 = (f32[4,8,256]{2,1,0:T(8,128)S(1)}, f32[4,8,256]{2,1,0:T(8,128)S(1)}, u32[]{:S(2)}, u32[]{:S(2)}) collective-permute-start(f32[4,8,256]{2,1,0:T(8,128)S(1)} %get-tuple-element.40), channel_id=1, source_target_pairs={{0,192},{8,200},{16,208},{24,216},{32,224},{40,232},{48,240},{56,2... | collective-permute-start | bytes 98312 | tf_op jit(solution)/shard_map/ppermute | solution.py:439
  48.4 1.2 %collective-permute-done.11.refs_2_ = f32[4,8,256]{2,1,0:T(8,128)S(1)} collective-permute-done((f32[4,8,256]{2,1,0:T(8,128)S(1)}, f32[4,8,256]{2,1,0:T(8,128)S(1)}, u32[]{:S(2)}, u32[]{:S(2)}) %collective-permute-start.11) | collective-permute-done | bytes 32800 | tf_op jit(solution)/shard_map/ppermute | solution.py:439
  49.6 0.9 %collective-permute-done.12.refs_3_ = f32[4,8,256]{2,1,0:T(8,128)S(1)} collective-permute-done((f32[4,8,256]{2,1,0:T(8,128)S(1)}, f32[4,8,256]{2,1,0:T(8,128)S(1)}, u32[]{:S(2)}, u32[]{:S(2)}) %collective-permute-start.12) | collective-permute-done | bytes 32800 | tf_op jit(solution)/shard_map/ppermute | solution.py:439
  50.5 0.6 %merge_y.1 = f32[4,8,256]{2,1,0:T(8,128)} custom-call(f32[4,8,256]{2,1,0:T(8,128)S(1)} %get-tuple-element.37.refs_0_, f32[4,8,256]{2,1,0:T(8,128)S(1)} %collective-permute-done.10.refs_1_, f32[4,8,256]{2,1,0:T(8,128)S(1)} %collective-permute-done.11.refs_2_, f32[4,8,256]{2,1,0:T(8,128)S(1)} %collective-permute-done.12.refs_3_), custom_call_target="tpu_custom_call" | custom-call | tf_op jit(solution)/shard_map/merge_y/pallas_call | solution.py:371
  (9 shorter events, 0.0 us)
Async XLA Ops:
  1.1 14.7 %collective-permute-start = (f32[256,256]{1,0:T(8,128)S(1)}, f32[256,256]{1,0:T(8,128)S(1)}, u32[]{:S(2)}, u32[]{:S(2)}) collective-permute-start(f32[256,256]{1,0:T(8,128)S(1)} %get-tuple-element.41.last_slab), channel_id=1, source_target_pairs={{0,8},{8,16},{16,24},{24,32},{32,40},{40,48},{48,56},{56,64},{64,7... | collective-permute-start | bytes 786440 | tf_op jit(solution)/shard_map/ppermute | solution.py:393
  3.1 12.7 %collective-permute-start.1 = (f32[256,256]{1,0:T(8,128)S(1)}, f32[256,256]{1,0:T(8,128)S(1)}, u32[]{:S(2)}, u32[]{:S(2)}) collective-permute-start(f32[256,256]{1,0:T(8,128)S(1)} %get-tuple-element.42.first_slab), channel_id=1, source_target_pairs={{8,0},{16,8},{24,16},{32,24},{40,32},{48,40},{56,48},{64,56},{72,6... | collective-permute-start | bytes 786440 | tf_op jit(solution)/shard_map/ppermute | solution.py:394
  12.3 3.2 %collective-permute-start.2 = (f32[4,8,128]{2,1,0:T(8,128)S(1)}, f32[4,8,128]{2,1,0:T(8,128)S(1)}, u32[]{:S(2)}, u32[]{:S(2)}) collective-permute-start(f32[4,8,128]{2,1,0:T(8,128)S(1)} %get-tuple-element.26), channel_id=1, source_target_pairs={{0,1},{1,2},{2,3},{3,4},{4,5},{5,6},{6,7},{7,0},{8,9},{9,10},{10,1... | collective-permute-start | bytes 49160 | tf_op jit(solution)/shard_map/ppermute | solution.py:402
  12.3 3.2 %collective-permute-start.3 = (f32[4,8,128]{2,1,0:T(8,128)S(1)}, f32[4,8,128]{2,1,0:T(8,128)S(1)}, u32[]{:S(2)}, u32[]{:S(2)}) collective-permute-start(f32[4,8,128]{2,1,0:T(8,128)S(1)} %get-tuple-element.27), channel_id=1, source_target_pairs={{1,0},{2,1},{3,2},{4,3},{5,4},{6,5},{7,6},{0,7},{9,8},{10,9},{11,1... | collective-permute-start | bytes 49160 | tf_op jit(solution)/shard_map/ppermute | solution.py:403
  18.9 9.2 %collective-permute-start.4 = (f32[2,4,4,8,256]{4,3,2,1,0:T(8,128)S(1)}, f32[2,4,4,8,256]{4,3,2,1,0:T(8,128)S(1)}, u32[]{:S(2)}, u32[]{:S(2)}) collective-permute-start(f32[2,4,4,8,256]{4,3,2,1,0:T(8,128)S(1)} %away.1.refs_0_), channel_id=1, source_target_pairs={{0,8},{8,0},{16,24},{24,16},{32,40},{40,32},{48,56},{56,48},{64,72... | collective-permute-start | bytes 786440 | tf_op jit(solution)/shard_map/ppermute | solution.py:406
  20.7 15.9 %collective-permute-start.6 = (f32[1,4,4,8,256]{4,3,2,1,0:T(8,128)S(1)}, f32[1,4,4,8,256]{4,3,2,1,0:T(8,128)S(1)}, u32[]{:S(2)}, u32[]{:S(2)}) collective-permute-start(f32[1,4,4,8,256]{4,3,2,1,0:T(8,128)S(1)} %near.1.refs_0_), channel_id=1, source_target_pairs={{0,56},{8,16},{16,8},{24,32},{32,24},{40,48},{48,40},{56,0},{64,12... | collective-permute-start | bytes 393224 | tf_op jit(solution)/shard_map/ppermute | solution.py:406
  23.8 12.7 %collective-permute-start.7 = (f32[1,4,4,8,256]{4,3,2,1,0:T(8,128)S(1)}, f32[1,4,4,8,256]{4,3,2,1,0:T(8,128)S(1)}, u32[]{:S(2)}, u32[]{:S(2)}) collective-permute-start(f32[1,4,4,8,256]{4,3,2,1,0:T(8,128)S(1)} %past.1.refs_1_), channel_id=1, source_target_pairs={{0,16},{8,56},{16,32},{24,8},{32,48},{40,24},{48,0},{56,40},{64,80... | collective-permute-start | bytes 393224 | tf_op jit(solution)/shard_map/ppermute | solution.py:406
  29.8 10.7 %collective-permute-start.8 = (f32[1,4,4,8,256]{4,3,2,1,0:T(8,128)S(1)}, f32[1,4,4,8,256]{4,3,2,1,0:T(8,128)S(1)}, u32[]{:S(2)}, u32[]{:S(2)}) collective-permute-start(f32[1,4,4,8,256]{4,3,2,1,0:T(8,128)S(1)} %keep3.1.refs_1_), channel_id=1, source_target_pairs={{0,40},{8,32},{16,56},{24,48},{32,8},{40,0},{48,24},{56,16},{64,10... | collective-permute-start | bytes 393224 | tf_op jit(solution)/shard_map/ppermute | solution.py:406
  32.7 8.9 %collective-permute-start.9 = (f32[1,4,4,8,256]{4,3,2,1,0:T(8,128)S(1)}, f32[1,4,4,8,256]{4,3,2,1,0:T(8,128)S(1)}, u32[]{:S(2)}, u32[]{:S(2)}) collective-permute-start(f32[1,4,4,8,256]{4,3,2,1,0:T(8,128)S(1)} %keep2.1.refs_0_), channel_id=1, source_target_pairs={{0,48},{8,24},{16,0},{24,40},{32,16},{40,56},{48,32},{56,8},{64,11... | collective-permute-start | bytes 393224 | tf_op jit(solution)/shard_map/ppermute | solution.py:406
  35.9 6.5 %collective-permute-start.5 = (f32[1,4,4,8,256]{4,3,2,1,0:T(8,128)S(1)}, f32[1,4,4,8,256]{4,3,2,1,0:T(8,128)S(1)}, u32[]{:S(2)}, u32[]{:S(2)}) collective-permute-start(f32[1,4,4,8,256]{4,3,2,1,0:T(8,128)S(1)} %mate.1.refs_0_), channel_id=1, source_target_pairs={{0,8},{8,0},{16,24},{24,16},{32,40},{40,32},{48,56},{56,48},{64,72... | collective-permute-start | bytes 393224 | tf_op jit(solution)/shard_map/ppermute | solution.py:406
  42.4 6.0 %collective-permute-start.10 = (f32[4,8,256]{2,1,0:T(8,128)S(1)}, f32[4,8,256]{2,1,0:T(8,128)S(1)}, u32[]{:S(2)}, u32[]{:S(2)}) collective-permute-start(f32[4,8,256]{2,1,0:T(8,128)S(1)} %get-tuple-element.38), channel_id=1, source_target_pairs={{0,64},{8,72},{16,80},{24,88},{32,96},{40,104},{48,112},{56,120},{... | collective-permute-start | bytes 98312 | tf_op jit(solution)/shard_map/ppermute | solution.py:439
  44.2 5.4 %collective-permute-start.11 = (f32[4,8,256]{2,1,0:T(8,128)S(1)}, f32[4,8,256]{2,1,0:T(8,128)S(1)}, u32[]{:S(2)}, u32[]{:S(2)}) collective-permute-start(f32[4,8,256]{2,1,0:T(8,128)S(1)} %get-tuple-element.39), channel_id=1, source_target_pairs={{0,128},{8,136},{16,144},{24,152},{32,160},{40,168},{48,176},{56,1... | collective-permute-start | bytes 98312 | tf_op jit(solution)/shard_map/ppermute | solution.py:439
  46.6 3.9 %collective-permute-start.12 = (f32[4,8,256]{2,1,0:T(8,128)S(1)}, f32[4,8,256]{2,1,0:T(8,128)S(1)}, u32[]{:S(2)}, u32[]{:S(2)}) collective-permute-start(f32[4,8,256]{2,1,0:T(8,128)S(1)} %get-tuple-element.40), channel_id=1, source_target_pairs={{0,192},{8,200},{16,208},{24,216},{32,224},{40,232},{48,240},{56,2... | collective-permute-start | bytes 98312 | tf_op jit(solution)/shard_map/ppermute | solution.py:439
